TPU v7x, 128 devices: a whole 4x4x4 slice. The times are simulated.
128 devices in a mesh: seg: 4 (over z), blk: 32 (over x, y, core).
Axes of the slice: x: 4, y: 4, z: 4, core: 2. Of those that a mesh axis runs over, the one named last changes fastest.
Arguments:
- records: float32 [12, 32768, 512], P('seg', 'blk'), may hold values from -600 to 600, as said below
- pairs: int32 [256, 8], P(('blk', 'seg')), may hold values from 0 to 1, as said below
Outputs:
- forward: float32 [256, 8, 65, 128], P(('blk', 'seg'))
- backward: float32 [256, 8, 65, 128], P(('blk', 'seg'))
Inputs may be any that keep to these rules, and one draw needn't show every extreme that they name: records are finite. pairs is 0 where g + d >= 256; among the 16 entries of rows 2 * o to 2 * o + 1 at most 8 are 1, and exactly 8 for some o.
All inputs are finite; a program needn't handle non-finite values.
Results may differ from a plain program's by a relative error of at most 0.0041.
Values may be sent and summed in bfloat16 or wider, within the bound.
No kernel may reach another device: no remote copies, remote signals or barrier semaphores. Data moves between devices by JAX's collectives and lax.ppermute only.
A program may use at most 192 MiB of HBM per device.

v0:
```python
import functools

import jax
import jax.numpy as jnp
import ml_dtypes
import numpy as np
from jax import lax
from jax.experimental import pallas as pl
from jax.experimental.pallas import tpu as pltpu
from jax.sharding import PartitionSpec as P

BINS = 256
LENGTH = 512
CHANS = 128
MAXLAG = 32
LAGS = 2 * MAXLAG + 1
REACH = 8
SMOOTH = 32
BAND = 64
GROUP = 8
HALF = GROUP // 2
PLANES = 4
ROWS = HALF * CHANS
SUB = ROWS
REACHED = 384
SLOTS = 13
SHIFTED = 8
BODY = 64
CHUNK = SLOTS * BODY + 16
SEND2 = SHIFTED * BODY + 16
SEND3 = 4 * BODY + 16
PAIRS, MOVES, WRITES, PLAN = 48, 8, 40, 128
TWO = CHUNK
THREE = CHUNK + SEND2
POOL = THREE + 3 * SEND3
MIB = 1024 * 1024
TINY = pl.CostEstimate(flops=1, bytes_accessed=1, transcendentals=0)
BF = jnp.bfloat16
F32 = jnp.float32
SMEM = pl.BlockSpec(memory_space=pltpu.SMEM)
VMEM = pl.BlockSpec(memory_space=pltpu.VMEM)


def split(array):
    high = array.astype(ml_dtypes.bfloat16)
    low = (array - high.astype(np.float32)).astype(ml_dtypes.bfloat16)
    return high, low


def lag_rows(segments):
    freqs = np.concatenate([np.arange(0, BINS, 2), np.arange(1, BINS, 2)])
    shifts = np.arange(-MAXLAG, MAXLAG + 1)
    phase = (shifts[:, None] * freqs[None, :] % LENGTH) * (2.0 * np.pi / LENGTH)
    table = np.concatenate([np.cos(phase), -np.sin(phase)], axis=1) / np.sqrt(segments * BINS)
    table = np.concatenate([table, np.zeros((CHANS - LAGS, LENGTH))], axis=0).T.astype(np.float32)
    return np.concatenate(split(table), axis=1)


def dot(a, b):
    return jnp.dot(a, b, preferred_element_type=F32)


def halves(x):
    high = x.astype(BF)
    return high, (x - high.astype(F32)).astype(BF)


def make_tables(tab):
    at = lax.broadcasted_iota(jnp.int32, (REACHED, LENGTH), 0)
    col = lax.broadcasted_iota(jnp.int32, (REACHED, LENGTH), 1)
    apart = at - col + jnp.where(col < BINS, 0, LENGTH - REACHED)
    tab[:REACHED] = jnp.where(jnp.abs(apart) <= SMOOTH, 1.0, 0.0).astype(BF)
    half = BINS // 2
    row = lax.broadcasted_iota(jnp.int32, (CHANS, LENGTH), 0)
    col = lax.broadcasted_iota(jnp.int32, (CHANS, LENGTH), 1)
    row = jnp.bitwise_and(row, half - 1) // (BAND // 2)
    col = jnp.bitwise_and(col, half - 1) // (BAND // 2)
    tab[REACHED:LENGTH] = jnp.where(row == col, 0.5 / BAND, 0.0).astype(BF)

    def cosine(step, shift):
        col = lax.broadcasted_iota(jnp.int32, (16, BINS), 1)
        freq = 2 * jnp.bitwise_and(col, half - 1) + jnp.right_shift(col, 7)
        k = lax.broadcasted_iota(jnp.int32, (16, BINS), 0) * freq
        k = jnp.bitwise_and(k * step - shift + BINS, LENGTH - 1) - BINS
        square = jnp.square(k.astype(F32) * (2.0 * np.pi / LENGTH))
        value = jnp.ones_like(square)
        for n in range(20, 0, -2):
            value = 1.0 - value * square * (1.0 / (n * (n - 1)))
        return value

    quarter = LENGTH // 4
    fine_cos, fine_sin = cosine(1, 0), cosine(1, quarter)
    coarse_cos, coarse_sin = cosine(16, 0), cosine(16, quarter)
    for a in range(16):
        c, s = coarse_cos[a : a + 1], coarse_sin[a : a + 1]
        for k, part in enumerate((c * fine_cos - s * fine_sin, -(s * fine_cos) - c * fine_sin)):
            for n, rounded in enumerate(halves(part)):
                rows = pl.ds(LENGTH + n * BINS + 16 * a, 16)
                tab[rows, k * half : (k + 1) * half] = rounded[:, :half]
                tab[rows, BINS + k * half : BINS + (k + 1) * half] = rounded[:, half:]


def whiten_body(outer, records, white, buf, tab, sems):
    segs = records.shape[0]
    core = jnp.bitwise_and(lax.axis_index("blk"), 1)
    begin = pl.multiple_of((core if outer else 1 - core) * ROWS, ROWS)

    def load(k):
        return pltpu.make_async_copy(records.at[k, pl.ds(begin, ROWS)], buf.at[k], sems.at[k])

    for k in range(segs):
        load(k).start()
    at = lax.broadcasted_iota(jnp.int32, (1, LENGTH), 1)
    count = jnp.minimum(at, SMOOTH) + jnp.minimum(LENGTH - 1 - at, SMOOTH) + 1
    share = 1.0 / count.astype(F32)
    make_tables(tab)

    def step(k, carry):
        load(k).wait()
        parts = range(ROWS // SUB)
        xs = [buf[k, pl.ds(n * SUB, SUB), :] for n in parts]
        levels = []
        first = tab[:REACHED, :BINS]
        second = tab[:REACHED, BINS:]
        for x in xs:
            ahi, alo = halves(jnp.abs(x))
            left = jnp.concatenate([ahi[:, :REACHED], alo[:, :REACHED]], axis=1)
            right = jnp.concatenate([ahi[:, LENGTH - REACHED :], alo[:, LENGTH - REACHED :]], axis=1)
            left = dot(left, jnp.concatenate([first, first], axis=0))
            right = dot(right, jnp.concatenate([second, second], axis=0))
            levels.append(jnp.concatenate([left, right], axis=1) * share)
        spectra = []
        products = []
        for at in (0, BINS):
            high = tab[LENGTH : LENGTH + BINS, at : at + BINS]
            products.append(jnp.concatenate([high, high, tab[LENGTH + BINS :, at : at + BINS]], axis=0))
        for x, level in zip(xs, levels):
            normed = x * pl.reciprocal(level + 1e-06, approx=True)
            left, right = normed[:, :BINS], normed[:, BINS:]
            pair = []
            for part, product in zip((left + right, left - right), products):
                high, low = halves(part)
                pair.append(dot(jnp.concatenate([high, low, high], axis=1), product))
            spectra.append(pair)
        same = jnp.concatenate([tab[REACHED:LENGTH, :BINS], tab[REACHED:LENGTH, BINS:]], axis=0)
        for n in parts:
            even, odd = spectra[n]
            re = jnp.concatenate([even[:, : BINS // 2], odd[:, : BINS // 2]], axis=1)
            im = jnp.concatenate([even[:, BINS // 2 :], odd[:, BINS // 2 :]], axis=1)
            power = dot((re * re + im * im).astype(BF), same)
            factor = lax.rsqrt(power + 1e-05)
            per = SUB // CHANS
            white[pl.ds(n * per, per), k, :, :BINS] = (re * factor).astype(BF).reshape(per, CHANS, BINS)
            white[pl.ds(n * per, per), k, :, BINS:] = (im * factor).astype(BF).reshape(per, CHANS, BINS)
        return carry

    lax.fori_loop(0, segs, step, 0)


def whiten(outer, records):
    segs = records.shape[0]
    return pl.pallas_call(
        functools.partial(whiten_body, outer),
        in_specs=[pl.BlockSpec(memory_space=pltpu.HBM)],
        out_specs=VMEM,
        out_shape=jax.ShapeDtypeStruct((HALF, segs, CHANS, LENGTH), BF),
        scratch_shapes=[
            pltpu.VMEM((segs, ROWS, LENGTH), F32),
            pltpu.VMEM((2 * LENGTH, LENGTH), BF),
            pltpu.SemaphoreType.DMA((segs,)),
        ],
        compiler_params=pltpu.CompilerParams(vmem_limit_bytes=50 * MIB),
        cost_estimate=TINY,
        name="whiten",
    )(records)


VISITS = [(p, d) for p in range(HALF) for d in range(1, REACH + 1) if p + d >= HALF] + [
    (p, d) for p in range(HALF, 12) for d in range(1, REACH + 1) if p < GROUP or p + d < 12
]
UPWARD = (
    ((0, 0), (1, 0), (1, 1), (2, 0), (2, 1), (3, 0), (3, 1)),
    ((2, 2), (3, 2), (3, 3)),
)


def seg_index():
    return lax.axis_index("seg").astype(jnp.int32)


def behind(owner):
    apart = jnp.bitwise_xor(seg_index(), owner)
    return 2 * jnp.bitwise_xor(apart, jnp.right_shift(apart, 1))


def list_pairs(own, before, codes, slots):
    s = seg_index()
    used = [jnp.int32(0)] * PLANES
    n = jnp.int32(0)
    for p, d in VISITS:
        row = p + HALF if p < HALF else p - HALF
        owner = row // 2
        live = (before if p < HALF else own)[behind(owner) + row % 2, d - 1]
        code = p + d * 16 + jnp.bitwise_xor(owner, s) * 256 + used[owner] * 4096
        slots[p * REACH + d - 1] = used[owner]
        used[owner] = used[owner] + live
        if p in (6, 7) and p + d in (12, 13):
            slots[96 + (p - 6) * 2 + p + d - 12] = used[0]
            code = code + (used[0] + 1) * 65536
            used[0] = used[0] + live
        codes[n] = code
        n = n + live
    return n


def plan_body(own, before, slots, plan):
    s = seg_index()
    n = jnp.int32(0)
    for owner in (0, 1):
        for k, (i, j) in enumerate(UPWARD[owner]):
            p, d = HALF + i, GROUP + j - i
            entry = p * REACH + d - 1 if i // 2 == owner else 96 + (i - 2) * 2 + j
            plan[MOVES + n] = slots[entry] + k * 4096
            n = n + jnp.where(s == owner, own[behind(i // 2) + i % 2, d - 1], 0)
    for r in range(1, PLANES):
        to = jnp.bitwise_xor(s, r)
        ahead = s < to
        for i in range(2):
            for j in range(2):
                row = 2 * s + i
                p = jnp.where(ahead, row + HALF, jnp.maximum(row - HALF, 0))
                d = 2 * to + j - row + jnp.where(ahead, 0, GROUP)
                live = jnp.where(ahead, own[i, d - 1], jnp.where(s >= 2, before[i, d - 1], 0))
                plan[MOVES + n] = slots[p * REACH + d - 1] + r * 256 + (2 * i + j) * 4096
                n = n + live
    plan[0] = n

    def write(n, i, d, base, size, slot):
        plan[WRITES + n] = base + slot * BODY + (base + size * BODY + slot) * 4096 + (i * 8 + d - 1) * 16777216

    n = jnp.int32(0)
    above = jnp.int32(0)
    for i in range(2):
        for d in range(1, REACH + 1):
            row = 2 * s + i
            live = own[i, d - 1]
            shift = (row + d >= GROUP) & (s >= 2)
            slot = jnp.where(shift, above, slots[(HALF + row) * REACH + d - 1])
            write(n, i, d, jnp.where(shift, TWO, 0), jnp.where(shift, SHIFTED, SLOTS), slot)
            n = n + live
            above = above + jnp.where(shift, live, 0)
    plan[1] = n
    for j in range(2):
        for d in range(1, REACH + 1):
            low = 2 * s + j - d
            crossing = low < 0
            row = jnp.where(crossing, low + GROUP, low)
            owner = jnp.right_shift(row, 1)
            at = behind(owner) + jnp.bitwise_and(row, 1)
            live = jnp.where(crossing, before[at, d - 1], own[at, d - 1])
            up = crossing & (owner < 2)
            mine = (owner == s) & jnp.logical_not(up)
            k0 = jnp.where(row == 0, 0, 2 * row - 1) + j
            k1 = jnp.where(row == 2, 0, 1) + j
            entry = jnp.maximum((HALF + low) * REACH + d - 1, 0)
            slot = jnp.where(mine, slots[entry], 2 * (row - 2 * owner) + j)
            slot = jnp.where(up, jnp.where(s == 0, k0, k1), slot)
            base = jnp.where(mine, 0, THREE + (jnp.bitwise_xor(s, owner) - 1) * SEND3)
            base = jnp.where(up, TWO, base)
            size = jnp.where(mine, SLOTS, jnp.where(up, SHIFTED, 4))
            write(n, j, d, base, size, slot)
            n = n + live
    plan[2] = n


def make_plan(*args):
    return pl.pallas_call(
        plan_body,
        in_specs=[SMEM] * 3,
        out_specs=SMEM,
        out_shape=jax.ShapeDtypeStruct((PLAN,), jnp.int32),
        compiler_params=pltpu.CompilerParams(vmem_limit_bytes=4 * MIB),
        cost_estimate=TINY,
        name="plan",
    )(*args)


def correlate_body(
    own, before, own_ext, own_int, got_ext, got_int, lag, keep, out1, out2, out3, slots, low, high, stk, pq, codes, last
):
    count = list_pairs(own, before, codes, slots)
    core = jnp.bitwise_and(lax.axis_index("blk"), 1)
    sources = (
        (own_ext, HALF * (1 + core)),
        (own_int, HALF * (2 - core)),
        (got_ext, 3 * HALF * core),
        (got_int, 3 * HALF * (1 - core)),
    )
    segs = low.shape[0]
    last[0] = -1

    def grab(dest, block):
        for ref, begin in sources:

            @pl.when((block >= begin) & (block < begin + HALF))
            def _(ref=ref, begin=begin):
                dest[...] = ref[block - begin]

    def put(r, n, stack):
        stk[r, pl.ds(pl.multiple_of(n * BODY, BODY), BODY), :] = stack[:BODY]
        stk[r, pl.ds(SLOTS * BODY + n, 1), :] = stack[BODY:LAGS]

    def pair(n, carry):
        code = codes[n]
        p = jnp.bitwise_and(code, 15)
        d = jnp.bitwise_and(jnp.right_shift(code, 4), 15)

        @pl.when(last[0] != p)
        def _():
            grab(low, p)
            last[0] = p

        grab(high, p + d)
        for chunk in range(CHANS // 16):
            rows = pl.ds(chunk * 16, 16)
            real = jnp.zeros((16, BINS), F32)
            imag = jnp.zeros((16, BINS), F32)
            for k in range(segs):
                are = low[k, rows, :BINS].astype(F32)
                aim = low[k, rows, BINS:].astype(F32)
                bre = high[k, rows, :BINS].astype(F32)
                bim = high[k, rows, BINS:].astype(F32)
                real += are * bre + aim * bim
                imag += are * bim - aim * bre
            rhi, rlo = halves(real)
            ihi, ilo = halves(imag)
            pq[0, rows, :BINS] = rhi
            pq[0, rows, BINS:] = ihi
            pq[1, rows, :BINS] = rlo
            pq[1, rows, BINS:] = ilo
        both = dot(pq[0], lag[...])
        stack = (both[:, :CHANS] + both[:, CHANS:] + dot(pq[1], lag[:, :CHANS])).T
        put(jnp.bitwise_and(jnp.right_shift(code, 8), 3), jnp.bitwise_and(jnp.right_shift(code, 12), 15), stack)
        second = jnp.right_shift(code, 16)

        @pl.when(second > 0)
        def _():
            put(seg_index(), second - 1, stack)

        return carry

    lax.fori_loop(0, count, pair, 0)
    keep[...] = stk[0]
    out1[...] = stk[1].astype(BF)
    out2[...] = stk[2].astype(BF)
    out3[...] = stk[3].astype(BF)


def correlate(own, before, whites, lag):
    segs = whites[0].shape[1]
    chunk = jax.ShapeDtypeStruct((CHUNK, CHANS), BF)
    return pl.pallas_call(
        correlate_body,
        in_specs=[SMEM] * 2 + [VMEM] * 5,
        out_specs=[VMEM] * 4 + [SMEM],
        out_shape=[
            jax.ShapeDtypeStruct((CHUNK, CHANS), F32),
            chunk,
            chunk,
            chunk,
            jax.ShapeDtypeStruct((128,), jnp.int32),
        ],
        scratch_shapes=[
            pltpu.VMEM((segs, CHANS, LENGTH), BF),
            pltpu.VMEM((segs, CHANS, LENGTH), BF),
            pltpu.VMEM((PLANES, CHUNK, CHANS), F32),
            pltpu.VMEM((2, CHANS, LENGTH), BF),
            pltpu.SMEM((PAIRS,), jnp.int32),
            pltpu.SMEM((1,), jnp.int32),
        ],
        compiler_params=pltpu.CompilerParams(vmem_limit_bytes=16 * MIB),
        cost_estimate=TINY,
        name="correlate",
    )(own, before, *whites, lag)


def combine_body(plan, keep, got2, got1, got3, full, send, out1, out2, out3, stage):
    full[...] = (keep[...] + got1[...].astype(F32)) + (got2[...].astype(F32) + got3[...].astype(F32))

    def move(n, carry):
        code = plan[MOVES + n]
        slot = jnp.bitwise_and(code, 255)
        message = jnp.bitwise_and(jnp.right_shift(code, 8), 15)
        k = jnp.right_shift(code, 12)
        size = jnp.where(message == 0, SHIFTED, 4)
        body = pl.ds(pl.multiple_of(slot * BODY, BODY), BODY)
        stage[message, pl.ds(pl.multiple_of(k * BODY, BODY), BODY), :] = full[body, :]
        stage[message, pl.ds(size * BODY + k, 1), :] = full[pl.ds(SLOTS * BODY + slot, 1), :]
        return carry

    lax.fori_loop(0, plan[0], move, 0)

    @pl.when(seg_index() >= 2)
    def _():
        send[: SHIFTED * BODY, :] = full[: SHIFTED * BODY, :].astype(BF)
        send[SHIFTED * BODY :, :] = full[SLOTS * BODY :, :].astype(BF)

    @pl.when(seg_index() < 2)
    def _():
        send[...] = stage[0].astype(BF)

    for r, out in ((1, out1), (2, out2), (3, out3)):
        out[...] = stage[r, :SEND3].astype(BF)


def combine(*args):
    third = jax.ShapeDtypeStruct((SEND3, CHANS), BF)
    return pl.pallas_call(
        combine_body,
        in_specs=[SMEM] + [VMEM] * 4,
        out_specs=[VMEM] * 5,
        out_shape=[
            jax.ShapeDtypeStruct((CHUNK, CHANS), F32),
            jax.ShapeDtypeStruct((SEND2, CHANS), BF),
            third,
            third,
            third,
        ],
        scratch_shapes=[pltpu.VMEM((PLANES, SEND2, CHANS), F32)],
        compiler_params=pltpu.CompilerParams(vmem_limit_bytes=8 * MIB),
        cost_estimate=TINY,
        name="combine",
    )(*args)


def finish_body(plan, full, got2, got1, got3, shifted, fwd, bwd, pool):
    pool[:TWO, :] = full[...]
    pool[TWO:THREE, :] = shifted[...].astype(F32)
    for r, got in ((1, got1), (2, got2), (3, got3)):
        pool[THREE + (r - 1) * SEND3 : THREE + r * SEND3, :] = got[...].astype(F32)
    fwd[...] = jnp.zeros(fwd.shape, F32)
    bwd[...] = jnp.zeros(bwd.shape, F32)

    def write(out, place, n):
        code = plan[WRITES + n]
        body = jnp.bitwise_and(code, 4095)
        i = jnp.right_shift(code, 27)
        at = pl.ds(jnp.bitwise_and(jnp.right_shift(code, 24), 7), 1)
        out[i, place(BODY), at, :] = pool[pl.ds(jnp.bitwise_and(jnp.right_shift(code, 12), 4095), 1), :]
        for m in range(BODY):
            out[i, place(m), at, :] = pool[pl.ds(body + m, 1), :]

    def ahead(n, carry):
        write(fwd, lambda m: m, n)
        return carry

    def behind(n, carry):
        write(bwd, lambda m: BODY - m, n)
        return carry

    lax.fori_loop(0, plan[1], ahead, 0)
    lax.fori_loop(plan[1], plan[2], behind, 0)


def finish(blocks, *args):
    out = jax.ShapeDtypeStruct((blocks, LAGS, REACH, CHANS), F32)
    return pl.pallas_call(
        finish_body,
        in_specs=[SMEM] + [VMEM] * 5,
        out_specs=[VMEM, VMEM],
        out_shape=[out, out],
        scratch_shapes=[pltpu.VMEM((POOL, CHANS), F32)],
        compiler_params=pltpu.CompilerParams(vmem_limit_bytes=8 * MIB),
        cost_estimate=TINY,
        name="finish",
    )(*args)


def shards(groups, planes, lag, records, pairs):
    def across(x, r):
        return lax.ppermute(x, "seg", [(z, z ^ r) for z in range(planes)])

    outer = [(g, g + 1 if g % 2 else g - 1) for g in range(1, groups - 1)]
    inner = [(g, g ^ 1) for g in range(groups)]
    upward = [(g, g + 1) for g in range(groups - 1)]
    shift = [
        (z * groups + g, z * groups + g + step)
        for z in range(planes)
        for g in range(groups)
        for step in (1 if z < 2 else -1,)
        if 0 <= g + step < groups
    ]
    own_ext = whiten(True, records)
    got_ext = lax.ppermute(own_ext, "blk", outer)
    own_int = whiten(False, records)
    got_int = lax.ppermute(own_int, "blk", inner)
    rows, _ = lax.optimization_barrier((pairs, own_int))
    own = jnp.concatenate([rows, across(rows, 1), across(rows, 3), across(rows, 2)])
    before = lax.ppermute(own, "blk", upward)

    keep, out1, out2, out3, slots = correlate(own, before, (own_ext, own_int, got_ext, got_int), lag)
    plan = make_plan(own, before, slots)
    full, send, out1, out2, out3 = combine(plan, keep, across(out2, 2), across(out1, 1), across(out3, 3))
    shifted = lax.ppermute(send, ("seg", "blk"), shift)
    outs = finish(pairs.shape[0], plan, full, across(out2, 2), across(out1, 1), across(out3, 3), shifted)
    return tuple(jnp.transpose(out, (0, 2, 1, 3)) for out in outs)


def solution(mesh):
    groups = mesh.shape["blk"]
    planes = mesh.shape["seg"]

    def run(records, pairs):
        body = functools.partial(
            shards,
            groups,
            planes,
            jnp.asarray(lag_rows(records.shape[0])),
        )
        return jax.shard_map(
            body,
            mesh=mesh,
            in_specs=(P("seg", "blk", None), P(("blk", "seg"), None)),
            out_specs=(P(("blk", "seg"), None, None, None), P(("blk", "seg"), None, None, None)),
            check_vma=False,
        )(records, pairs)

    return run
```

profile of v0, /device:TPU:6, one launch (start us, length us, event | category | flops | bytes accessed | tf_op | source)
XLA Modules:
  0.0 64.2 jit_solution(2178329590505103133)
XLA Ops:
  0.6 4.9 %whiten.3.own_ext = bf16[4,3,128,512]{3,2,1,0:T(8,128)(2,1)S(1)} custom-call(f32[3,1024,512]{2,1,0:T(8,128)} %records.3), custom_call_target="tpu_custom_call" | custom-call | flops 1 | bytes 1 | tf_op jit(solution)/shard_map/whiten/pallas_call | solution.py:162
  5.5 0.0 copy-start.1
  5.5 0.0 copy-start
  5.6 4.8 %collective-permute-start.4 = (bf16[4,3,128,512]{3,2,1,0:T(8,128)(2,1)S(1)}, bf16[4,3,128,512]{3,2,1,0:T(8,128)(2,1)S(1)}, u32[]{:S(2)}, u32[]{:S(2)}) collective-permute-start(bf16[4,3,128,512]{3,2,1,0:T(8,128)(2,1)S(1)} %whiten.3.own_ext), channel_id=1, source_target_pairs={{1,2},{2,1},{3,4},{4,3},{5,6},{6,5},{7,8},{8,7},{9,10},{10,9},{11,... | collective-permute-start | bytes 4718600 | tf_op jit(solution)/shard_map/ppermute | solution.py:494
  10.3 4.9 %whiten.2.own_int = bf16[4,3,128,512]{3,2,1,0:T(8,128)(2,1)S(1)} custom-call(f32[3,1024,512]{2,1,0:T(8,128)} %records.3), custom_call_target="tpu_custom_call" | custom-call | flops 1 | bytes 1 | tf_op jit(solution)/shard_map/whiten/pallas_call | solution.py:162
  15.2 0.1 collective-permute-start.5
  15.3 0.0 copy-done.1
  15.3 4.0 %collective-permute-start.2 = (s32[2,8]{1,0:T(2,128)S(1)}, s32[2,8]{1,0:T(2,128)S(1)}, u32[]{:S(2)}, u32[]{:S(2)}) collective-permute-start(s32[2,8]{1,0:T(2,128)S(1)} %copy-done.1), channel_id=1, source_target_pairs={{0,64},{32,96},{64,0},{96,32},{1,65},{33,97},{65,1},{97,33},{2,66}... | collective-permute-start | bytes 200 | tf_op jit(solution)/shard_map/ppermute | solution.py:481
  19.3 0.7 %collective-permute-start.1 = (s32[2,8]{1,0:T(2,128)S(1)}, s32[2,8]{1,0:T(2,128)S(1)}, u32[]{:S(2)}, u32[]{:S(2)}) collective-permute-start(s32[2,8]{1,0:T(2,128)S(1)} %copy-done.1), channel_id=1, source_target_pairs={{0,96},{32,64},{64,32},{96,0},{1,97},{33,65},{65,33},{97,1},{2,98}... | collective-permute-start | bytes 200 | tf_op jit(solution)/shard_map/ppermute | solution.py:481
  20.0 0.3 collective-permute-start
  20.3 0.5 collective-permute-done.2
  20.8 3.2 %collective-permute-done.1 = s32[2,8]{1,0:T(2,128)S(1)} collective-permute-done((s32[2,8]{1,0:T(2,128)S(1)}, s32[2,8]{1,0:T(2,128)S(1)}, u32[]{:S(2)}, u32[]{:S(2)}) %collective-permute-start.1) | collective-permute-done | bytes 96 | tf_op jit(solution)/shard_map/ppermute | solution.py:481
  24.1 0.0 collective-permute-done
  24.1 1.9 %collective-permute-start.3 = (s32[8,8]{1,0:T(8,128)S(1)}, s32[8,8]{1,0:T(8,128)S(1)}, u32[]{:S(2)}, u32[]{:S(2)}) collective-permute-start(s32[8,8]{1,0:T(8,128)S(1)} %pad_add_fusion.own), channel_id=1, source_target_pairs={{0,1},{1,2},{2,3},{3,4},{4,5},{5,6},{6,7},{7,8},{8,9},{9,10},{10,1... | collective-permute-start | bytes 776 | tf_op jit(solution)/shard_map/ppermute | solution.py:499
  26.0 5.1 %collective-permute-done.3.before = s32[8,8]{1,0:T(8,128)S(1)} collective-permute-done((s32[8,8]{1,0:T(8,128)S(1)}, s32[8,8]{1,0:T(8,128)S(1)}, u32[]{:S(2)}, u32[]{:S(2)}) %collective-permute-start.3) | collective-permute-done | bytes 288 | tf_op jit(solution)/shard_map/ppermute | solution.py:499
  31.1 0.0 collective-permute-done.4.got_ext
  31.1 0.0 collective-permute-done.5.got_int
  31.1 0.0 copy-done
  31.1 4.2 %correlate.1 = (f32[848,128]{1,0:T(8,128)S(1)}, bf16[848,128]{1,0:T(8,128)(2,1)S(1)}, bf16[848,128]{1,0:T(8,128)(2,1)S(1)}, bf16[848,128]{1,0:T(8,128)(2,1)S(1)}, s32[128]{0:T(128)S(1)}) custom-call(s32[8,8]{1,0:T(8,128)S(1)} %pad_add_fusion.own, s32[8,8]{1,0:T(8,128)S(1)} %collective-permute-done.3.before, bf16[4,3,128,512]{3,2,1,0:T(8,128)(2,1)S(1)} %whiten.3.own_ext, ...), custom_call_target="tpu_custom_call" | custom-call | flops 1 | bytes 1 | tf_op jit(solution)/shard_map/correlate/pallas_call | solution.py:362
  35.4 2.4 %collective-permute-start.6 = (bf16[848,128]{1,0:T(8,128)(2,1)S(1)}, bf16[848,128]{1,0:T(8,128)(2,1)S(1)}, u32[]{:S(2)}, u32[]{:S(2)}) collective-permute-start(bf16[848,128]{1,0:T(8,128)(2,1)S(1)} %get-tuple-element.18), channel_id=1, source_target_pairs={{0,64},{32,96},{64,0},{96,32},{1,65},{33,97},{65,1},{97,33},{2,66}... | collective-permute-start | bytes 651272 | tf_op jit(solution)/shard_map/ppermute | solution.py:481
  37.8 1.0 %collective-permute-start.7 = (bf16[848,128]{1,0:T(8,128)(2,1)S(1)}, bf16[848,128]{1,0:T(8,128)(2,1)S(1)}, u32[]{:S(2)}, u32[]{:S(2)}) collective-permute-start(bf16[848,128]{1,0:T(8,128)(2,1)S(1)} %get-tuple-element.19), channel_id=1, source_target_pairs={{0,32},{32,0},{64,96},{96,64},{1,33},{33,1},{65,97},{97,65},{2,34}... | collective-permute-start | bytes 651272 | tf_op jit(solution)/shard_map/ppermute | solution.py:481
  38.8 0.7 %collective-permute-start.8 = (bf16[848,128]{1,0:T(8,128)(2,1)S(1)}, bf16[848,128]{1,0:T(8,128)(2,1)S(1)}, u32[]{:S(2)}, u32[]{:S(2)}) collective-permute-start(bf16[848,128]{1,0:T(8,128)(2,1)S(1)} %get-tuple-element.20), channel_id=1, source_target_pairs={{0,96},{32,64},{64,32},{96,0},{1,97},{33,65},{65,33},{97,1},{2,98}... | collective-permute-start | bytes 651272 | tf_op jit(solution)/shard_map/ppermute | solution.py:481
  39.5 1.7 %plan.1 = s32[128]{0:T(128)S(1)} custom-call(s32[8,8]{1,0:T(8,128)S(1)} %pad_add_fusion.own, s32[8,8]{1,0:T(8,128)S(1)} %collective-permute-done.3.before, s32[128]{0:T(128)S(1)} %get-tuple-element.16.slots), custom_call_target="tpu_custom_call" | custom-call | flops 1 | bytes 1 | tf_op jit(solution)/shard_map/plan/pallas_call | solution.py:277
  41.2 3.0 %collective-permute-done.6.got2 = bf16[848,128]{1,0:T(8,128)(2,1)S(1)} collective-permute-done((bf16[848,128]{1,0:T(8,128)(2,1)S(1)}, bf16[848,128]{1,0:T(8,128)(2,1)S(1)}, u32[]{:S(2)}, u32[]{:S(2)}) %collective-permute-start.6) | collective-permute-done | bytes 217120 | tf_op jit(solution)/shard_map/ppermute | solution.py:481
  44.2 3.0 %collective-permute-done.7.got1 = bf16[848,128]{1,0:T(8,128)(2,1)S(1)} collective-permute-done((bf16[848,128]{1,0:T(8,128)(2,1)S(1)}, bf16[848,128]{1,0:T(8,128)(2,1)S(1)}, u32[]{:S(2)}, u32[]{:S(2)}) %collective-permute-start.7) | collective-permute-done | bytes 217120 | tf_op jit(solution)/shard_map/ppermute | solution.py:481
  47.2 0.3 collective-permute-done.8.got3
  47.5 0.7 %combine.1 = (f32[848,128]{1,0:T(8,128)S(1)}, bf16[528,128]{1,0:T(8,128)(2,1)S(1)}, bf16[272,128]{1,0:T(8,128)(2,1)S(1)}, bf16[272,128]{1,0:T(8,128)(2,1)S(1)}, bf16[272,128]{1,0:T(8,128)(2,1)S(1)}) custom-call(s32[128]{0:T(128)S(1)} %plan.1, f32[848,128]{1,0:T(8,128)S(1)} %get-tuple-element.17.keep, bf16[848,128]{1,0:T(8,128)(2,1)S(1)} %collective-permute-done.6.got2, ...), custom_call_target="tpu_custom_call" | custom-call | flops 1 | bytes 1 | tf_op jit(solution)/shard_map/combine/pallas_call | solution.py:418
  48.2 1.9 %collective-permute-start.12 = (bf16[528,128]{1,0:T(8,128)(2,1)S(1)}, bf16[528,128]{1,0:T(8,128)(2,1)S(1)}, u32[]{:S(2)}, u32[]{:S(2)}) collective-permute-start(bf16[528,128]{1,0:T(8,128)(2,1)S(1)} %get-tuple-element.25), channel_id=1, source_target_pairs={{0,1},{1,2},{2,3},{3,4},{4,5},{5,6},{6,7},{7,8},{8,9},{9,10},{10,1... | collective-permute-start | bytes 405512 | tf_op jit(solution)/shard_map/ppermute | solution.py:504
  50.1 5.7 %collective-permute-start.9 = (bf16[272,128]{1,0:T(8,128)(2,1)S(1)}, bf16[272,128]{1,0:T(8,128)(2,1)S(1)}, u32[]{:S(2)}, u32[]{:S(2)}) collective-permute-start(bf16[272,128]{1,0:T(8,128)(2,1)S(1)} %get-tuple-element.22), channel_id=1, source_target_pairs={{0,64},{32,96},{64,0},{96,32},{1,65},{33,97},{65,1},{97,33},{2,66}... | collective-permute-start | bytes 208904 | tf_op jit(solution)/shard_map/ppermute | solution.py:481
  55.9 1.1 %collective-permute-start.10 = (bf16[272,128]{1,0:T(8,128)(2,1)S(1)}, bf16[272,128]{1,0:T(8,128)(2,1)S(1)}, u32[]{:S(2)}, u32[]{:S(2)}) collective-permute-start(bf16[272,128]{1,0:T(8,128)(2,1)S(1)} %get-tuple-element.23), channel_id=1, source_target_pairs={{0,32},{32,0},{64,96},{96,64},{1,33},{33,1},{65,97},{97,65},{2,34}... | collective-permute-start | bytes 208904 | tf_op jit(solution)/shard_map/ppermute | solution.py:481
  56.9 0.0 collective-permute-start.11
  56.9 1.3 %collective-permute-done.9.got2 = bf16[272,128]{1,0:T(8,128)(2,1)S(1)} collective-permute-done((bf16[272,128]{1,0:T(8,128)(2,1)S(1)}, bf16[272,128]{1,0:T(8,128)(2,1)S(1)}, u32[]{:S(2)}, u32[]{:S(2)}) %collective-permute-start.9) | collective-permute-done | bytes 69664 | tf_op jit(solution)/shard_map/ppermute | solution.py:481
  58.3 1.9 %collective-permute-done.10.got1 = bf16[272,128]{1,0:T(8,128)(2,1)S(1)} collective-permute-done((bf16[272,128]{1,0:T(8,128)(2,1)S(1)}, bf16[272,128]{1,0:T(8,128)(2,1)S(1)}, u32[]{:S(2)}, u32[]{:S(2)}) %collective-permute-start.10) | collective-permute-done | bytes 69664 | tf_op jit(solution)/shard_map/ppermute | solution.py:481
  60.2 2.3 %collective-permute-done.11.got3 = bf16[272,128]{1,0:T(8,128)(2,1)S(1)} collective-permute-done((bf16[272,128]{1,0:T(8,128)(2,1)S(1)}, bf16[272,128]{1,0:T(8,128)(2,1)S(1)}, u32[]{:S(2)}, u32[]{:S(2)}) %collective-permute-start.11) | collective-permute-done | bytes 69664 | tf_op jit(solution)/shard_map/ppermute | solution.py:481
  62.5 0.0 collective-permute-done.12.shifted
  62.5 1.8 %finish.1 = (f32[2,65,8,128]{3,2,1,0:T(8,128)}, f32[2,65,8,128]{3,2,1,0:T(8,128)}) custom-call(s32[128]{0:T(128)S(1)} %plan.1, f32[848,128]{1,0:T(8,128)S(1)} %get-tuple-element.21.full, bf16[272,128]{1,0:T(8,128)(2,1)S(1)} %collective-permute-done.9.got2, bf16[272,128]{1,0:T(8,128)(2,1)S(1)} %collective-permute-done.10.got1, ...), custom_call_target="tpu_custom_call" | custom-call | flops 1 | bytes 1 | tf_op jit(solution)/shard_map/finish/pallas_call | solution.py:467
  (1 shorter events, 0.0 us)
Async XLA Ops:
  5.5 9.8 %copy-start.1 = (s32[2,8]{1,0:T(2,128)S(1)}, s32[2,8]{1,0:T(2,128)}, u32[]{:S(2)}) copy-start(s32[2,8]{1,0:T(2,128)} %param.4) | copy-start | bytes 196
  5.5 25.6 %copy-start = (bf16[512,256]{1,0:T(8,128)(2,1)S(1)}, bf16[512,256]{1,0:T(8,128)(2,1)}, u32[]{:S(2)}) copy-start(bf16[512,256]{1,0:T(8,128)(2,1)} %constant.2.clone.lag) | copy-start | bytes 786436
  5.6 25.6 %collective-permute-start.4 = (bf16[4,3,128,512]{3,2,1,0:T(8,128)(2,1)S(1)}, bf16[4,3,128,512]{3,2,1,0:T(8,128)(2,1)S(1)}, u32[]{:S(2)}, u32[]{:S(2)}) collective-permute-start(bf16[4,3,128,512]{3,2,1,0:T(8,128)(2,1)S(1)} %whiten.3.own_ext), channel_id=1, source_target_pairs={{1,2},{2,1},{3,4},{4,3},{5,6},{6,5},{7,8},{8,7},{9,10},{10,9},{11,... | collective-permute-start | bytes 4718600 | tf_op jit(solution)/shard_map/ppermute | solution.py:494
  15.2 15.9 %collective-permute-start.5 = (bf16[4,3,128,512]{3,2,1,0:T(8,128)(2,1)S(1)}, bf16[4,3,128,512]{3,2,1,0:T(8,128)(2,1)S(1)}, u32[]{:S(2)}, u32[]{:S(2)}) collective-permute-start(bf16[4,3,128,512]{3,2,1,0:T(8,128)(2,1)S(1)} %whiten.2.own_int), channel_id=1, source_target_pairs={{0,1},{1,0},{2,3},{3,2},{4,5},{5,4},{6,7},{7,6},{8,9},{9,8},{10,11... | collective-permute-start | bytes 4718600 | tf_op jit(solution)/shard_map/ppermute | solution.py:496
  15.3 5.5 %collective-permute-start.2 = (s32[2,8]{1,0:T(2,128)S(1)}, s32[2,8]{1,0:T(2,128)S(1)}, u32[]{:S(2)}, u32[]{:S(2)}) collective-permute-start(s32[2,8]{1,0:T(2,128)S(1)} %copy-done.1), channel_id=1, source_target_pairs={{0,64},{32,96},{64,0},{96,32},{1,65},{33,97},{65,1},{97,33},{2,66}... | collective-permute-start | bytes 200 | tf_op jit(solution)/shard_map/ppermute | solution.py:481
  19.3 4.8 %collective-permute-start.1 = (s32[2,8]{1,0:T(2,128)S(1)}, s32[2,8]{1,0:T(2,128)S(1)}, u32[]{:S(2)}, u32[]{:S(2)}) collective-permute-start(s32[2,8]{1,0:T(2,128)S(1)} %copy-done.1), channel_id=1, source_target_pairs={{0,96},{32,64},{64,32},{96,0},{1,97},{33,65},{65,33},{97,1},{2,98}... | collective-permute-start | bytes 200 | tf_op jit(solution)/shard_map/ppermute | solution.py:481
  20.0 4.1 %collective-permute-start = (s32[2,8]{1,0:T(2,128)S(1)}, s32[2,8]{1,0:T(2,128)S(1)}, u32[]{:S(2)}, u32[]{:S(2)}) collective-permute-start(s32[2,8]{1,0:T(2,128)S(1)} %copy-done.1), channel_id=1, source_target_pairs={{0,32},{32,0},{64,96},{96,64},{1,33},{33,1},{65,97},{97,65},{2,34}... | collective-permute-start | bytes 200 | tf_op jit(solution)/shard_map/ppermute | solution.py:481
  24.1 7.0 %collective-permute-start.3 = (s32[8,8]{1,0:T(8,128)S(1)}, s32[8,8]{1,0:T(8,128)S(1)}, u32[]{:S(2)}, u32[]{:S(2)}) collective-permute-start(s32[8,8]{1,0:T(8,128)S(1)} %pad_add_fusion.own), channel_id=1, source_target_pairs={{0,1},{1,2},{2,3},{3,4},{4,5},{5,6},{6,7},{7,8},{8,9},{9,10},{10,1... | collective-permute-start | bytes 776 | tf_op jit(solution)/shard_map/ppermute | solution.py:499
  35.4 8.8 %collective-permute-start.6 = (bf16[848,128]{1,0:T(8,128)(2,1)S(1)}, bf16[848,128]{1,0:T(8,128)(2,1)S(1)}, u32[]{:S(2)}, u32[]{:S(2)}) collective-permute-start(bf16[848,128]{1,0:T(8,128)(2,1)S(1)} %get-tuple-element.18), channel_id=1, source_target_pairs={{0,64},{32,96},{64,0},{96,32},{1,65},{33,97},{65,1},{97,33},{2,66}... | collective-permute-start | bytes 651272 | tf_op jit(solution)/shard_map/ppermute | solution.py:481
  37.8 9.4 %collective-permute-start.7 = (bf16[848,128]{1,0:T(8,128)(2,1)S(1)}, bf16[848,128]{1,0:T(8,128)(2,1)S(1)}, u32[]{:S(2)}, u32[]{:S(2)}) collective-permute-start(bf16[848,128]{1,0:T(8,128)(2,1)S(1)} %get-tuple-element.19), channel_id=1, source_target_pairs={{0,32},{32,0},{64,96},{96,64},{1,33},{33,1},{65,97},{97,65},{2,34}... | collective-permute-start | bytes 651272 | tf_op jit(solution)/shard_map/ppermute | solution.py:481
  38.8 8.7 %collective-permute-start.8 = (bf16[848,128]{1,0:T(8,128)(2,1)S(1)}, bf16[848,128]{1,0:T(8,128)(2,1)S(1)}, u32[]{:S(2)}, u32[]{:S(2)}) collective-permute-start(bf16[848,128]{1,0:T(8,128)(2,1)S(1)} %get-tuple-element.20), channel_id=1, source_target_pairs={{0,96},{32,64},{64,32},{96,0},{1,97},{33,65},{65,33},{97,1},{2,98}... | collective-permute-start | bytes 651272 | tf_op jit(solution)/shard_map/ppermute | solution.py:481
  48.2 14.2 %collective-permute-start.12 = (bf16[528,128]{1,0:T(8,128)(2,1)S(1)}, bf16[528,128]{1,0:T(8,128)(2,1)S(1)}, u32[]{:S(2)}, u32[]{:S(2)}) collective-permute-start(bf16[528,128]{1,0:T(8,128)(2,1)S(1)} %get-tuple-element.25), channel_id=1, source_target_pairs={{0,1},{1,2},{2,3},{3,4},{4,5},{5,6},{6,7},{7,8},{8,9},{9,10},{10,1... | collective-permute-start | bytes 405512 | tf_op jit(solution)/shard_map/ppermute | solution.py:504
  50.1 8.1 %collective-permute-start.9 = (bf16[272,128]{1,0:T(8,128)(2,1)S(1)}, bf16[272,128]{1,0:T(8,128)(2,1)S(1)}, u32[]{:S(2)}, u32[]{:S(2)}) collective-permute-start(bf16[272,128]{1,0:T(8,128)(2,1)S(1)} %get-tuple-element.22), channel_id=1, source_target_pairs={{0,64},{32,96},{64,0},{96,32},{1,65},{33,97},{65,1},{97,33},{2,66}... | collective-permute-start | bytes 208904 | tf_op jit(solution)/shard_map/ppermute | solution.py:481
  55.9 4.3 %collective-permute-start.10 = (bf16[272,128]{1,0:T(8,128)(2,1)S(1)}, bf16[272,128]{1,0:T(8,128)(2,1)S(1)}, u32[]{:S(2)}, u32[]{:S(2)}) collective-permute-start(bf16[272,128]{1,0:T(8,128)(2,1)S(1)} %get-tuple-element.23), channel_id=1, source_target_pairs={{0,32},{32,0},{64,96},{96,64},{1,33},{33,1},{65,97},{97,65},{2,34}... | collective-permute-start | bytes 208904 | tf_op jit(solution)/shard_map/ppermute | solution.py:481
  56.9 5.5 %collective-permute-start.11 = (bf16[272,128]{1,0:T(8,128)(2,1)S(1)}, bf16[272,128]{1,0:T(8,128)(2,1)S(1)}, u32[]{:S(2)}, u32[]{:S(2)}) collective-permute-start(bf16[272,128]{1,0:T(8,128)(2,1)S(1)} %get-tuple-element.24), channel_id=1, source_target_pairs={{0,96},{32,64},{64,32},{96,0},{1,97},{33,65},{65,33},{97,1},{2,98}... | collective-permute-start | bytes 208904 | tf_op jit(solution)/shard_map/ppermute | solution.py:481
where the time goes:
time: 64.9 us; the launch traced here: 64.2 us
  starting transfers between devices  24.6 us (38%)
  waiting for transfers between devices  20.7 us (32%)
  Pallas kernels  18.2 us (28%)
  between operations  0.74 us (1%)
    ppermute x9, starting transfers between devices, across(): return lax.ppermute(x, 'seg', [(z, z ^ r) for z in range(planes)])  16 us
    ppermute x9, waiting for transfers between devices, across(): return lax.ppermute(x, 'seg', [(z, z ^ r) for z in range(planes)])  15.5 us
    pallas_call x2, Pallas kernels, whiten(): pl.pallas_call(functools.partial(whiten_body, outer), in_specs=[pl.BlockS...  9.78 us
    ppermute x1, waiting for transfers between devices, shards(): before = lax.ppermute(own, 'blk', upward)  5.11 us
    ppermute x1, starting transfers between devices, shards(): got_ext = lax.ppermute(own_ext, 'blk', outer)  4.76 us
    pallas_call x1, Pallas kernels, correlate(): pl.pallas_call(correlate_body, in_specs=[SMEM] * 2 + [VMEM] * 5, out_spec...  4.22 us
    ppermute x1, starting transfers between devices, shards(): before = lax.ppermute(own, 'blk', upward)  1.92 us
    ppermute x1, starting transfers between devices, shards(): shifted = lax.ppermute(send, ('seg', 'blk'), shift)  1.92 us
  transfers between devices with their start and end apart: 13, of which 9 were waited for; matrix products, arithmetic and copies ran while one was open for 0% of the time, Pallas kernels for 10%

commit v1 on v0

--- a/solution.py
+++ b/solution.py
@@ -384,7 +384,7 @@
     )(own, before, *whites, lag)
 
 
-def combine_body(plan, keep, got2, got1, got3, full, send, out1, out2, out3, stage):
+def combine_body(plan, keep, got1, got3, got2, full, send, out1, out2, out3, stage):
     full[...] = (keep[...] + got1[...].astype(F32)) + (got2[...].astype(F32) + got3[...].astype(F32))
 
     def move(n, carry):
@@ -500,7 +500,7 @@
 
     keep, out1, out2, out3, slots = correlate(own, before, (own_ext, own_int, got_ext, got_int), lag)
     plan = make_plan(own, before, slots)
-    full, send, out1, out2, out3 = combine(plan, keep, across(out2, 2), across(out1, 1), across(out3, 3))
+    full, send, out1, out2, out3 = combine(plan, keep, across(out1, 1), across(out3, 3), across(out2, 2))
     shifted = lax.ppermute(send, ("seg", "blk"), shift)
     outs = finish(pairs.shape[0], plan, full, across(out2, 2), across(out1, 1), across(out3, 3), shifted)
     return tuple(jnp.transpose(out, (0, 2, 1, 3)) for out in outs)

time: 64.9 us -> 64.8 us (level)
  the two profiles are of different devices: /device:TPU:6 before, /device:TPU:2 now
where the time goes in v1:
time: 64.8 us; the launch traced here: 64.2 us
  starting transfers between devices  22.8 us (35%)
  Pallas kernels  21.6 us (33%)
  waiting for transfers between devices  19 us (29%)
  between operations  0.75 us (1%)
    ppermute x9, starting transfers between devices, across(): return lax.ppermute(x, 'seg', [(z, z ^ r) for z in range(planes)])  14.4 us
    ppermute x9, waiting for transfers between devices, across(): return lax.ppermute(x, 'seg', [(z, z ^ r) for z in range(planes)])  13.9 us
    pallas_call x2, Pallas kernels, whiten(): pl.pallas_call(functools.partial(whiten_body, outer), in_specs=[pl.BlockS...  9.79 us
    pallas_call x1, Pallas kernels, correlate(): pl.pallas_call(correlate_body, in_specs=[SMEM] * 2 + [VMEM] * 5, out_spec...  7.56 us
    ppermute x1, waiting for transfers between devices, shards(): before = lax.ppermute(own, 'blk', upward)  5.11 us
    ppermute x1, starting transfers between devices, shards(): got_ext = lax.ppermute(own_ext, 'blk', outer)  4.46 us
    ppermute x1, starting transfers between devices, shards(): before = lax.ppermute(own, 'blk', upward)  1.92 us
    ppermute x1, starting transfers between devices, shards(): shifted = lax.ppermute(send, ('seg', 'blk'), shift)  1.92 us
  transfers between devices with their start and end apart: 13, of which 8 were waited for; matrix products, arithmetic and copies ran while one was open for 0% of the time, Pallas kernels for 10%

profile of v1, /device:TPU:2, one launch (start us, length us, event | category | flops | bytes accessed | tf_op | source)
XLA Modules:
  0.0 64.2 jit_solution(18199590080992592763)
XLA Ops:
  0.6 4.9 %whiten.3.own_ext = bf16[4,3,128,512]{3,2,1,0:T(8,128)(2,1)S(1)} custom-call(f32[3,1024,512]{2,1,0:T(8,128)} %records.3), custom_call_target="tpu_custom_call" | custom-call | flops 1 | bytes 1 | tf_op jit(solution)/shard_map/whiten/pallas_call | solution.py:162
  5.5 0.0 copy-start.1
  5.5 0.0 copy-start
  5.6 4.5 %collective-permute-start.4 = (bf16[4,3,128,512]{3,2,1,0:T(8,128)(2,1)S(1)}, bf16[4,3,128,512]{3,2,1,0:T(8,128)(2,1)S(1)}, u32[]{:S(2)}, u32[]{:S(2)}) collective-permute-start(bf16[4,3,128,512]{3,2,1,0:T(8,128)(2,1)S(1)} %whiten.3.own_ext), channel_id=1, source_target_pairs={{1,2},{2,1},{3,4},{4,3},{5,6},{6,5},{7,8},{8,7},{9,10},{10,9},{11,... | collective-permute-start | bytes 4718600 | tf_op jit(solution)/shard_map/ppermute | solution.py:494
  10.0 4.9 %whiten.2.own_int = bf16[4,3,128,512]{3,2,1,0:T(8,128)(2,1)S(1)} custom-call(f32[3,1024,512]{2,1,0:T(8,128)} %records.3), custom_call_target="tpu_custom_call" | custom-call | flops 1 | bytes 1 | tf_op jit(solution)/shard_map/whiten/pallas_call | solution.py:162
  14.9 0.1 collective-permute-start.5
  15.0 0.0 copy-done.1
  15.0 4.0 %collective-permute-start.2 = (s32[2,8]{1,0:T(2,128)S(1)}, s32[2,8]{1,0:T(2,128)S(1)}, u32[]{:S(2)}, u32[]{:S(2)}) collective-permute-start(s32[2,8]{1,0:T(2,128)S(1)} %copy-done.1), channel_id=1, source_target_pairs={{0,64},{32,96},{64,0},{96,32},{1,65},{33,97},{65,1},{97,33},{2,66}... | collective-permute-start | bytes 200 | tf_op jit(solution)/shard_map/ppermute | solution.py:481
  19.0 0.7 %collective-permute-start.1 = (s32[2,8]{1,0:T(2,128)S(1)}, s32[2,8]{1,0:T(2,128)S(1)}, u32[]{:S(2)}, u32[]{:S(2)}) collective-permute-start(s32[2,8]{1,0:T(2,128)S(1)} %copy-done.1), channel_id=1, source_target_pairs={{0,96},{32,64},{64,32},{96,0},{1,97},{33,65},{65,33},{97,1},{2,98}... | collective-permute-start | bytes 200 | tf_op jit(solution)/shard_map/ppermute | solution.py:481
  19.7 0.3 collective-permute-start
  20.0 0.5 collective-permute-done.2
  20.5 3.2 %collective-permute-done.1 = s32[2,8]{1,0:T(2,128)S(1)} collective-permute-done((s32[2,8]{1,0:T(2,128)S(1)}, s32[2,8]{1,0:T(2,128)S(1)}, u32[]{:S(2)}, u32[]{:S(2)}) %collective-permute-start.1) | collective-permute-done | bytes 96 | tf_op jit(solution)/shard_map/ppermute | solution.py:481
  23.8 0.0 collective-permute-done
  23.8 1.9 %collective-permute-start.3 = (s32[8,8]{1,0:T(8,128)S(1)}, s32[8,8]{1,0:T(8,128)S(1)}, u32[]{:S(2)}, u32[]{:S(2)}) collective-permute-start(s32[8,8]{1,0:T(8,128)S(1)} %pad_add_fusion.own), channel_id=1, source_target_pairs={{0,1},{1,2},{2,3},{3,4},{4,5},{5,6},{6,7},{7,8},{8,9},{9,10},{10,1... | collective-permute-start | bytes 776 | tf_op jit(solution)/shard_map/ppermute | solution.py:499
  25.7 5.1 %collective-permute-done.3.before = s32[8,8]{1,0:T(8,128)S(1)} collective-permute-done((s32[8,8]{1,0:T(8,128)S(1)}, s32[8,8]{1,0:T(8,128)S(1)}, u32[]{:S(2)}, u32[]{:S(2)}) %collective-permute-start.3) | collective-permute-done | bytes 288 | tf_op jit(solution)/shard_map/ppermute | solution.py:499
  30.8 0.0 collective-permute-done.4.got_ext
  30.8 0.0 collective-permute-done.5.got_int
  30.8 0.0 copy-done
  30.8 7.6 %correlate.1 = (f32[848,128]{1,0:T(8,128)S(1)}, bf16[848,128]{1,0:T(8,128)(2,1)S(1)}, bf16[848,128]{1,0:T(8,128)(2,1)S(1)}, bf16[848,128]{1,0:T(8,128)(2,1)S(1)}, s32[128]{0:T(128)S(1)}) custom-call(s32[8,8]{1,0:T(8,128)S(1)} %pad_add_fusion.own, s32[8,8]{1,0:T(8,128)S(1)} %collective-permute-done.3.before, bf16[4,3,128,512]{3,2,1,0:T(8,128)(2,1)S(1)} %whiten.3.own_ext, ...), custom_call_target="tpu_custom_call" | custom-call | flops 1 | bytes 1 | tf_op jit(solution)/shard_map/correlate/pallas_call | solution.py:362
  38.4 0.7 %collective-permute-start.6 = (bf16[848,128]{1,0:T(8,128)(2,1)S(1)}, bf16[848,128]{1,0:T(8,128)(2,1)S(1)}, u32[]{:S(2)}, u32[]{:S(2)}) collective-permute-start(bf16[848,128]{1,0:T(8,128)(2,1)S(1)} %get-tuple-element.18), channel_id=1, source_target_pairs={{0,32},{32,0},{64,96},{96,64},{1,33},{33,1},{65,97},{97,65},{2,34}... | collective-permute-start | bytes 651272 | tf_op jit(solution)/shard_map/ppermute | solution.py:481
  39.2 2.5 %collective-permute-start.7 = (bf16[848,128]{1,0:T(8,128)(2,1)S(1)}, bf16[848,128]{1,0:T(8,128)(2,1)S(1)}, u32[]{:S(2)}, u32[]{:S(2)}) collective-permute-start(bf16[848,128]{1,0:T(8,128)(2,1)S(1)} %get-tuple-element.19), channel_id=1, source_target_pairs={{0,96},{32,64},{64,32},{96,0},{1,97},{33,65},{65,33},{97,1},{2,98}... | collective-permute-start | bytes 651272 | tf_op jit(solution)/shard_map/ppermute | solution.py:481
  41.7 1.1 %collective-permute-start.8 = (bf16[848,128]{1,0:T(8,128)(2,1)S(1)}, bf16[848,128]{1,0:T(8,128)(2,1)S(1)}, u32[]{:S(2)}, u32[]{:S(2)}) collective-permute-start(bf16[848,128]{1,0:T(8,128)(2,1)S(1)} %get-tuple-element.20), channel_id=1, source_target_pairs={{0,64},{32,96},{64,0},{96,32},{1,65},{33,97},{65,1},{97,33},{2,66}... | collective-permute-start | bytes 651272 | tf_op jit(solution)/shard_map/ppermute | solution.py:481
  42.7 1.7 %plan.1 = s32[128]{0:T(128)S(1)} custom-call(s32[8,8]{1,0:T(8,128)S(1)} %pad_add_fusion.own, s32[8,8]{1,0:T(8,128)S(1)} %collective-permute-done.3.before, s32[128]{0:T(128)S(1)} %get-tuple-element.16.slots), custom_call_target="tpu_custom_call" | custom-call | flops 1 | bytes 1 | tf_op jit(solution)/shard_map/plan/pallas_call | solution.py:277
  44.4 0.0 collective-permute-done.6.got1
  44.4 3.0 %collective-permute-done.7.got3 = bf16[848,128]{1,0:T(8,128)(2,1)S(1)} collective-permute-done((bf16[848,128]{1,0:T(8,128)(2,1)S(1)}, bf16[848,128]{1,0:T(8,128)(2,1)S(1)}, u32[]{:S(2)}, u32[]{:S(2)}) %collective-permute-start.7) | collective-permute-done | bytes 217120 | tf_op jit(solution)/shard_map/ppermute | solution.py:481
  47.4 1.6 %collective-permute-done.8.got2 = bf16[848,128]{1,0:T(8,128)(2,1)S(1)} collective-permute-done((bf16[848,128]{1,0:T(8,128)(2,1)S(1)}, bf16[848,128]{1,0:T(8,128)(2,1)S(1)}, u32[]{:S(2)}, u32[]{:S(2)}) %collective-permute-start.8) | collective-permute-done | bytes 217120 | tf_op jit(solution)/shard_map/ppermute | solution.py:481
  49.1 0.8 %combine.1 = (f32[848,128]{1,0:T(8,128)S(1)}, bf16[528,128]{1,0:T(8,128)(2,1)S(1)}, bf16[272,128]{1,0:T(8,128)(2,1)S(1)}, bf16[272,128]{1,0:T(8,128)(2,1)S(1)}, bf16[272,128]{1,0:T(8,128)(2,1)S(1)}) custom-call(s32[128]{0:T(128)S(1)} %plan.1, f32[848,128]{1,0:T(8,128)S(1)} %get-tuple-element.17.keep, bf16[848,128]{1,0:T(8,128)(2,1)S(1)} %collective-permute-done.6.got1, ...), custom_call_target="tpu_custom_call" | custom-call | flops 1 | bytes 1 | tf_op jit(solution)/shard_map/combine/pallas_call | solution.py:418
  49.8 1.9 %collective-permute-start.12 = (bf16[528,128]{1,0:T(8,128)(2,1)S(1)}, bf16[528,128]{1,0:T(8,128)(2,1)S(1)}, u32[]{:S(2)}, u32[]{:S(2)}) collective-permute-start(bf16[528,128]{1,0:T(8,128)(2,1)S(1)} %get-tuple-element.25), channel_id=1, source_target_pairs={{0,1},{1,2},{2,3},{3,4},{4,5},{5,6},{6,7},{7,8},{8,9},{9,10},{10,1... | collective-permute-start | bytes 405512 | tf_op jit(solution)/shard_map/ppermute | solution.py:504
  51.8 4.1 %collective-permute-start.9 = (bf16[272,128]{1,0:T(8,128)(2,1)S(1)}, bf16[272,128]{1,0:T(8,128)(2,1)S(1)}, u32[]{:S(2)}, u32[]{:S(2)}) collective-permute-start(bf16[272,128]{1,0:T(8,128)(2,1)S(1)} %get-tuple-element.22), channel_id=1, source_target_pairs={{0,64},{32,96},{64,0},{96,32},{1,65},{33,97},{65,1},{97,33},{2,66}... | collective-permute-start | bytes 208904 | tf_op jit(solution)/shard_map/ppermute | solution.py:481
  55.8 1.0 %collective-permute-start.10 = (bf16[272,128]{1,0:T(8,128)(2,1)S(1)}, bf16[272,128]{1,0:T(8,128)(2,1)S(1)}, u32[]{:S(2)}, u32[]{:S(2)}) collective-permute-start(bf16[272,128]{1,0:T(8,128)(2,1)S(1)} %get-tuple-element.23), channel_id=1, source_target_pairs={{0,32},{32,0},{64,96},{96,64},{1,33},{33,1},{65,97},{97,65},{2,34}... | collective-permute-start | bytes 208904 | tf_op jit(solution)/shard_map/ppermute | solution.py:481
  56.9 0.0 collective-permute-start.11
  56.9 2.0 %collective-permute-done.9.got2 = bf16[272,128]{1,0:T(8,128)(2,1)S(1)} collective-permute-done((bf16[272,128]{1,0:T(8,128)(2,1)S(1)}, bf16[272,128]{1,0:T(8,128)(2,1)S(1)}, u32[]{:S(2)}, u32[]{:S(2)}) %collective-permute-start.9) | collective-permute-done | bytes 69664 | tf_op jit(solution)/shard_map/ppermute | solution.py:481
  58.9 1.3 %collective-permute-done.10.got1 = bf16[272,128]{1,0:T(8,128)(2,1)S(1)} collective-permute-done((bf16[272,128]{1,0:T(8,128)(2,1)S(1)}, bf16[272,128]{1,0:T(8,128)(2,1)S(1)}, u32[]{:S(2)}, u32[]{:S(2)}) %collective-permute-start.10) | collective-permute-done | bytes 69664 | tf_op jit(solution)/shard_map/ppermute | solution.py:481
  60.2 2.2 %collective-permute-done.11.got3 = bf16[272,128]{1,0:T(8,128)(2,1)S(1)} collective-permute-done((bf16[272,128]{1,0:T(8,128)(2,1)S(1)}, bf16[272,128]{1,0:T(8,128)(2,1)S(1)}, u32[]{:S(2)}, u32[]{:S(2)}) %collective-permute-start.11) | collective-permute-done | bytes 69664 | tf_op jit(solution)/shard_map/ppermute | solution.py:481
  62.4 0.0 collective-permute-done.12.shifted
  62.4 1.9 %finish.1 = (f32[2,65,8,128]{3,2,1,0:T(8,128)}, f32[2,65,8,128]{3,2,1,0:T(8,128)}) custom-call(s32[128]{0:T(128)S(1)} %plan.1, f32[848,128]{1,0:T(8,128)S(1)} %get-tuple-element.21.full, bf16[272,128]{1,0:T(8,128)(2,1)S(1)} %collective-permute-done.9.got2, bf16[272,128]{1,0:T(8,128)(2,1)S(1)} %collective-permute-done.10.got1, ...), custom_call_target="tpu_custom_call" | custom-call | flops 1 | bytes 1 | tf_op jit(solution)/shard_map/finish/pallas_call | solution.py:467
  (1 shorter events, 0.0 us)
Async XLA Ops:
  5.5 9.5 %copy-start.1 = (s32[2,8]{1,0:T(2,128)S(1)}, s32[2,8]{1,0:T(2,128)}, u32[]{:S(2)}) copy-start(s32[2,8]{1,0:T(2,128)} %param.4) | copy-start | bytes 196
  5.5 25.3 %copy-start = (bf16[512,256]{1,0:T(8,128)(2,1)S(1)}, bf16[512,256]{1,0:T(8,128)(2,1)}, u32[]{:S(2)}) copy-start(bf16[512,256]{1,0:T(8,128)(2,1)} %constant.2.clone.lag) | copy-start | bytes 786436
  5.6 25.3 %collective-permute-start.4 = (bf16[4,3,128,512]{3,2,1,0:T(8,128)(2,1)S(1)}, bf16[4,3,128,512]{3,2,1,0:T(8,128)(2,1)S(1)}, u32[]{:S(2)}, u32[]{:S(2)}) collective-permute-start(bf16[4,3,128,512]{3,2,1,0:T(8,128)(2,1)S(1)} %whiten.3.own_ext), channel_id=1, source_target_pairs={{1,2},{2,1},{3,4},{4,3},{5,6},{6,5},{7,8},{8,7},{9,10},{10,9},{11,... | collective-permute-start | bytes 4718600 | tf_op jit(solution)/shard_map/ppermute | solution.py:494
  14.9 15.9 %collective-permute-start.5 = (bf16[4,3,128,512]{3,2,1,0:T(8,128)(2,1)S(1)}, bf16[4,3,128,512]{3,2,1,0:T(8,128)(2,1)S(1)}, u32[]{:S(2)}, u32[]{:S(2)}) collective-permute-start(bf16[4,3,128,512]{3,2,1,0:T(8,128)(2,1)S(1)} %whiten.2.own_int), channel_id=1, source_target_pairs={{0,1},{1,0},{2,3},{3,2},{4,5},{5,4},{6,7},{7,6},{8,9},{9,8},{10,11... | collective-permute-start | bytes 4718600 | tf_op jit(solution)/shard_map/ppermute | solution.py:496
  15.0 5.5 %collective-permute-start.2 = (s32[2,8]{1,0:T(2,128)S(1)}, s32[2,8]{1,0:T(2,128)S(1)}, u32[]{:S(2)}, u32[]{:S(2)}) collective-permute-start(s32[2,8]{1,0:T(2,128)S(1)} %copy-done.1), channel_id=1, source_target_pairs={{0,64},{32,96},{64,0},{96,32},{1,65},{33,97},{65,1},{97,33},{2,66}... | collective-permute-start | bytes 200 | tf_op jit(solution)/shard_map/ppermute | solution.py:481
  19.0 4.8 %collective-permute-start.1 = (s32[2,8]{1,0:T(2,128)S(1)}, s32[2,8]{1,0:T(2,128)S(1)}, u32[]{:S(2)}, u32[]{:S(2)}) collective-permute-start(s32[2,8]{1,0:T(2,128)S(1)} %copy-done.1), channel_id=1, source_target_pairs={{0,96},{32,64},{64,32},{96,0},{1,97},{33,65},{65,33},{97,1},{2,98}... | collective-permute-start | bytes 200 | tf_op jit(solution)/shard_map/ppermute | solution.py:481
  19.7 4.1 %collective-permute-start = (s32[2,8]{1,0:T(2,128)S(1)}, s32[2,8]{1,0:T(2,128)S(1)}, u32[]{:S(2)}, u32[]{:S(2)}) collective-permute-start(s32[2,8]{1,0:T(2,128)S(1)} %copy-done.1), channel_id=1, source_target_pairs={{0,32},{32,0},{64,96},{96,64},{1,33},{33,1},{65,97},{97,65},{2,34}... | collective-permute-start | bytes 200 | tf_op jit(solution)/shard_map/ppermute | solution.py:481
  23.8 7.0 %collective-permute-start.3 = (s32[8,8]{1,0:T(8,128)S(1)}, s32[8,8]{1,0:T(8,128)S(1)}, u32[]{:S(2)}, u32[]{:S(2)}) collective-permute-start(s32[8,8]{1,0:T(8,128)S(1)} %pad_add_fusion.own), channel_id=1, source_target_pairs={{0,1},{1,2},{2,3},{3,4},{4,5},{5,6},{6,7},{7,8},{8,9},{9,10},{10,1... | collective-permute-start | bytes 776 | tf_op jit(solution)/shard_map/ppermute | solution.py:499
  38.4 6.0 %collective-permute-start.6 = (bf16[848,128]{1,0:T(8,128)(2,1)S(1)}, bf16[848,128]{1,0:T(8,128)(2,1)S(1)}, u32[]{:S(2)}, u32[]{:S(2)}) collective-permute-start(bf16[848,128]{1,0:T(8,128)(2,1)S(1)} %get-tuple-element.18), channel_id=1, source_target_pairs={{0,32},{32,0},{64,96},{96,64},{1,33},{33,1},{65,97},{97,65},{2,34}... | collective-permute-start | bytes 651272 | tf_op jit(solution)/shard_map/ppermute | solution.py:481
  39.2 8.3 %collective-permute-start.7 = (bf16[848,128]{1,0:T(8,128)(2,1)S(1)}, bf16[848,128]{1,0:T(8,128)(2,1)S(1)}, u32[]{:S(2)}, u32[]{:S(2)}) collective-permute-start(bf16[848,128]{1,0:T(8,128)(2,1)S(1)} %get-tuple-element.19), channel_id=1, source_target_pairs={{0,96},{32,64},{64,32},{96,0},{1,97},{33,65},{65,33},{97,1},{2,98}... | collective-permute-start | bytes 651272 | tf_op jit(solution)/shard_map/ppermute | solution.py:481
  41.7 7.4 %collective-permute-start.8 = (bf16[848,128]{1,0:T(8,128)(2,1)S(1)}, bf16[848,128]{1,0:T(8,128)(2,1)S(1)}, u32[]{:S(2)}, u32[]{:S(2)}) collective-permute-start(bf16[848,128]{1,0:T(8,128)(2,1)S(1)} %get-tuple-element.20), channel_id=1, source_target_pairs={{0,64},{32,96},{64,0},{96,32},{1,65},{33,97},{65,1},{97,33},{2,66}... | collective-permute-start | bytes 651272 | tf_op jit(solution)/shard_map/ppermute | solution.py:481
  49.8 12.6 %collective-permute-start.12 = (bf16[528,128]{1,0:T(8,128)(2,1)S(1)}, bf16[528,128]{1,0:T(8,128)(2,1)S(1)}, u32[]{:S(2)}, u32[]{:S(2)}) collective-permute-start(bf16[528,128]{1,0:T(8,128)(2,1)S(1)} %get-tuple-element.25), channel_id=1, source_target_pairs={{0,1},{1,2},{2,3},{3,4},{4,5},{5,6},{6,7},{7,8},{8,9},{9,10},{10,1... | collective-permute-start | bytes 405512 | tf_op jit(solution)/shard_map/ppermute | solution.py:504
  51.8 7.1 %collective-permute-start.9 = (bf16[272,128]{1,0:T(8,128)(2,1)S(1)}, bf16[272,128]{1,0:T(8,128)(2,1)S(1)}, u32[]{:S(2)}, u32[]{:S(2)}) collective-permute-start(bf16[272,128]{1,0:T(8,128)(2,1)S(1)} %get-tuple-element.22), channel_id=1, source_target_pairs={{0,64},{32,96},{64,0},{96,32},{1,65},{33,97},{65,1},{97,33},{2,66}... | collective-permute-start | bytes 208904 | tf_op jit(solution)/shard_map/ppermute | solution.py:481
  55.8 4.3 %collective-permute-start.10 = (bf16[272,128]{1,0:T(8,128)(2,1)S(1)}, bf16[272,128]{1,0:T(8,128)(2,1)S(1)}, u32[]{:S(2)}, u32[]{:S(2)}) collective-permute-start(bf16[272,128]{1,0:T(8,128)(2,1)S(1)} %get-tuple-element.23), channel_id=1, source_target_pairs={{0,32},{32,0},{64,96},{96,64},{1,33},{33,1},{65,97},{97,65},{2,34}... | collective-permute-start | bytes 208904 | tf_op jit(solution)/shard_map/ppermute | solution.py:481
  56.9 5.5 %collective-permute-start.11 = (bf16[272,128]{1,0:T(8,128)(2,1)S(1)}, bf16[272,128]{1,0:T(8,128)(2,1)S(1)}, u32[]{:S(2)}, u32[]{:S(2)}) collective-permute-start(bf16[272,128]{1,0:T(8,128)(2,1)S(1)} %get-tuple-element.24), channel_id=1, source_target_pairs={{0,96},{32,64},{64,32},{96,0},{1,97},{33,65},{65,33},{97,1},{2,98}... | collective-permute-start | bytes 208904 | tf_op jit(solution)/shard_map/ppermute | solution.py:481

commit v2 on v1

--- a/solution.py
+++ b/solution.py
@@ -410,7 +410,7 @@
         send[...] = stage[0].astype(BF)
 
     for r, out in ((1, out1), (2, out2), (3, out3)):
-        out[...] = stage[r, :SEND3].astype(BF)
+        out[:SEND3, :] = stage[r, :SEND3].astype(BF)
 
 
 def combine(*args):
@@ -423,7 +423,7 @@
             jax.ShapeDtypeStruct((CHUNK, CHANS), F32),
             jax.ShapeDtypeStruct((SEND2, CHANS), BF),
             third,
-            third,
+            jax.ShapeDtypeStruct((SEND2, CHANS), BF),
             third,
         ],
         scratch_shapes=[pltpu.VMEM((PLANES, SEND2, CHANS), F32)],
@@ -433,11 +433,11 @@
     )(*args)
 
 
-def finish_body(plan, full, got2, got1, got3, shifted, fwd, bwd, pool):
+def finish_body(plan, full, got2, shifted, got1, got3, fwd, bwd, pool):
     pool[:TWO, :] = full[...]
     pool[TWO:THREE, :] = shifted[...].astype(F32)
     for r, got in ((1, got1), (2, got2), (3, got3)):
-        pool[THREE + (r - 1) * SEND3 : THREE + r * SEND3, :] = got[...].astype(F32)
+        pool[THREE + (r - 1) * SEND3 : THREE + r * SEND3, :] = got[:SEND3, :].astype(F32)
     fwd[...] = jnp.zeros(fwd.shape, F32)
     bwd[...] = jnp.zeros(bwd.shape, F32)
 
@@ -502,7 +502,7 @@
     plan = make_plan(own, before, slots)
     full, send, out1, out2, out3 = combine(plan, keep, across(out1, 1), across(out3, 3), across(out2, 2))
     shifted = lax.ppermute(send, ("seg", "blk"), shift)
-    outs = finish(pairs.shape[0], plan, full, across(out2, 2), across(out1, 1), across(out3, 3), shifted)
+    outs = finish(pairs.shape[0], plan, full, across(out2, 2), shifted, across(out1, 1), across(out3, 3))
     return tuple(jnp.transpose(out, (0, 2, 1, 3)) for out in outs)
 
 

time: 64.8 us -> 63 us (0.972)
  the two profiles are of different devices: /device:TPU:2 before, /device:TPU:6 now
where the time goes in v2:
time: 63 us; the launch traced here: 62.7 us
  starting transfers between devices  25.2 us (40%)
  Pallas kernels  18.7 us (30%)
  waiting for transfers between devices  18 us (29%)
  between operations  0.74 us (1%)
    ppermute x9, starting transfers between devices, across(): return lax.ppermute(x, 'seg', [(z, z ^ r) for z in range(planes)])  16.6 us
    ppermute x9, waiting for transfers between devices, across(): return lax.ppermute(x, 'seg', [(z, z ^ r) for z in range(planes)])  12.9 us
    pallas_call x2, Pallas kernels, whiten(): pl.pallas_call(functools.partial(whiten_body, outer), in_specs=[pl.BlockS...  9.78 us
    ppermute x1, waiting for transfers between devices, shards(): before = lax.ppermute(own, 'blk', upward)  5.11 us
    ppermute x1, starting transfers between devices, shards(): got_ext = lax.ppermute(own_ext, 'blk', outer)  4.76 us
    pallas_call x1, Pallas kernels, correlate(): pl.pallas_call(correlate_body, in_specs=[SMEM] * 2 + [VMEM] * 5, out_spec...  4.63 us
    ppermute x1, starting transfers between devices, shards(): before = lax.ppermute(own, 'blk', upward)  1.92 us
    ppermute x1, starting transfers between devices, shards(): shifted = lax.ppermute(send, ('seg', 'blk'), shift)  1.91 us
  transfers between devices with their start and end apart: 13, of which 7 were waited for; matrix products, arithmetic and copies ran while one was open for 0% of the time, Pallas kernels for 10%

profile of v2, /device:TPU:6, one launch (start us, length us, event | category | flops | bytes accessed | tf_op | source)
XLA Modules:
  0.0 62.7 jit_solution(2908045485519831446)
XLA Ops:
  0.6 4.9 %whiten.3.own_ext = bf16[4,3,128,512]{3,2,1,0:T(8,128)(2,1)S(1)} custom-call(f32[3,1024,512]{2,1,0:T(8,128)} %records.3), custom_call_target="tpu_custom_call" | custom-call | flops 1 | bytes 1 | tf_op jit(solution)/shard_map/whiten/pallas_call | solution.py:162
  5.5 0.0 copy-start.1
  5.5 0.0 copy-start
  5.6 4.8 %collective-permute-start.4 = (bf16[4,3,128,512]{3,2,1,0:T(8,128)(2,1)S(1)}, bf16[4,3,128,512]{3,2,1,0:T(8,128)(2,1)S(1)}, u32[]{:S(2)}, u32[]{:S(2)}) collective-permute-start(bf16[4,3,128,512]{3,2,1,0:T(8,128)(2,1)S(1)} %whiten.3.own_ext), channel_id=1, source_target_pairs={{1,2},{2,1},{3,4},{4,3},{5,6},{6,5},{7,8},{8,7},{9,10},{10,9},{11,... | collective-permute-start | bytes 4718600 | tf_op jit(solution)/shard_map/ppermute | solution.py:494
  10.3 4.9 %whiten.2.own_int = bf16[4,3,128,512]{3,2,1,0:T(8,128)(2,1)S(1)} custom-call(f32[3,1024,512]{2,1,0:T(8,128)} %records.3), custom_call_target="tpu_custom_call" | custom-call | flops 1 | bytes 1 | tf_op jit(solution)/shard_map/whiten/pallas_call | solution.py:162
  15.2 0.1 collective-permute-start.5
  15.3 0.0 copy-done.1
  15.3 4.0 %collective-permute-start.2 = (s32[2,8]{1,0:T(2,128)S(1)}, s32[2,8]{1,0:T(2,128)S(1)}, u32[]{:S(2)}, u32[]{:S(2)}) collective-permute-start(s32[2,8]{1,0:T(2,128)S(1)} %copy-done.1), channel_id=1, source_target_pairs={{0,64},{32,96},{64,0},{96,32},{1,65},{33,97},{65,1},{97,33},{2,66}... | collective-permute-start | bytes 200 | tf_op jit(solution)/shard_map/ppermute | solution.py:481
  19.3 0.7 %collective-permute-start.1 = (s32[2,8]{1,0:T(2,128)S(1)}, s32[2,8]{1,0:T(2,128)S(1)}, u32[]{:S(2)}, u32[]{:S(2)}) collective-permute-start(s32[2,8]{1,0:T(2,128)S(1)} %copy-done.1), channel_id=1, source_target_pairs={{0,96},{32,64},{64,32},{96,0},{1,97},{33,65},{65,33},{97,1},{2,98}... | collective-permute-start | bytes 200 | tf_op jit(solution)/shard_map/ppermute | solution.py:481
  20.0 0.3 collective-permute-start
  20.3 0.5 collective-permute-done.2
  20.8 3.2 %collective-permute-done.1 = s32[2,8]{1,0:T(2,128)S(1)} collective-permute-done((s32[2,8]{1,0:T(2,128)S(1)}, s32[2,8]{1,0:T(2,128)S(1)}, u32[]{:S(2)}, u32[]{:S(2)}) %collective-permute-start.1) | collective-permute-done | bytes 96 | tf_op jit(solution)/shard_map/ppermute | solution.py:481
  24.1 0.0 collective-permute-done
  24.1 1.9 %collective-permute-start.3 = (s32[8,8]{1,0:T(8,128)S(1)}, s32[8,8]{1,0:T(8,128)S(1)}, u32[]{:S(2)}, u32[]{:S(2)}) collective-permute-start(s32[8,8]{1,0:T(8,128)S(1)} %pad_add_fusion.own), channel_id=1, source_target_pairs={{0,1},{1,2},{2,3},{3,4},{4,5},{5,6},{6,7},{7,8},{8,9},{9,10},{10,1... | collective-permute-start | bytes 776 | tf_op jit(solution)/shard_map/ppermute | solution.py:499
  26.0 5.1 %collective-permute-done.3.before = s32[8,8]{1,0:T(8,128)S(1)} collective-permute-done((s32[8,8]{1,0:T(8,128)S(1)}, s32[8,8]{1,0:T(8,128)S(1)}, u32[]{:S(2)}, u32[]{:S(2)}) %collective-permute-start.3) | collective-permute-done | bytes 288 | tf_op jit(solution)/shard_map/ppermute | solution.py:499
  31.1 0.0 collective-permute-done.4.got_ext
  31.1 0.0 collective-permute-done.5.got_int
  31.1 0.0 copy-done
  31.1 4.6 %correlate.1 = (f32[848,128]{1,0:T(8,128)S(1)}, bf16[848,128]{1,0:T(8,128)(2,1)S(1)}, bf16[848,128]{1,0:T(8,128)(2,1)S(1)}, bf16[848,128]{1,0:T(8,128)(2,1)S(1)}, s32[128]{0:T(128)S(1)}) custom-call(s32[8,8]{1,0:T(8,128)S(1)} %pad_add_fusion.own, s32[8,8]{1,0:T(8,128)S(1)} %collective-permute-done.3.before, bf16[4,3,128,512]{3,2,1,0:T(8,128)(2,1)S(1)} %whiten.3.own_ext, ...), custom_call_target="tpu_custom_call" | custom-call | flops 1 | bytes 1 | tf_op jit(solution)/shard_map/correlate/pallas_call | solution.py:362
  35.8 0.5 collective-permute-start.6
  36.2 2.5 %collective-permute-start.7 = (bf16[848,128]{1,0:T(8,128)(2,1)S(1)}, bf16[848,128]{1,0:T(8,128)(2,1)S(1)}, u32[]{:S(2)}, u32[]{:S(2)}) collective-permute-start(bf16[848,128]{1,0:T(8,128)(2,1)S(1)} %get-tuple-element.19), channel_id=1, source_target_pairs={{0,96},{32,64},{64,32},{96,0},{1,97},{33,65},{65,33},{97,1},{2,98}... | collective-permute-start | bytes 651272 | tf_op jit(solution)/shard_map/ppermute | solution.py:481
  38.7 1.2 %collective-permute-start.8 = (bf16[848,128]{1,0:T(8,128)(2,1)S(1)}, bf16[848,128]{1,0:T(8,128)(2,1)S(1)}, u32[]{:S(2)}, u32[]{:S(2)}) collective-permute-start(bf16[848,128]{1,0:T(8,128)(2,1)S(1)} %get-tuple-element.20), channel_id=1, source_target_pairs={{0,64},{32,96},{64,0},{96,32},{1,65},{33,97},{65,1},{97,33},{2,66}... | collective-permute-start | bytes 651272 | tf_op jit(solution)/shard_map/ppermute | solution.py:481
  39.9 1.7 %plan.1 = s32[128]{0:T(128)S(1)} custom-call(s32[8,8]{1,0:T(8,128)S(1)} %pad_add_fusion.own, s32[8,8]{1,0:T(8,128)S(1)} %collective-permute-done.3.before, s32[128]{0:T(128)S(1)} %get-tuple-element.16.slots), custom_call_target="tpu_custom_call" | custom-call | flops 1 | bytes 1 | tf_op jit(solution)/shard_map/plan/pallas_call | solution.py:277
  41.6 1.8 %collective-permute-done.6.got1 = bf16[848,128]{1,0:T(8,128)(2,1)S(1)} collective-permute-done((bf16[848,128]{1,0:T(8,128)(2,1)S(1)}, bf16[848,128]{1,0:T(8,128)(2,1)S(1)}, u32[]{:S(2)}, u32[]{:S(2)}) %collective-permute-start.6) | collective-permute-done | bytes 217120 | tf_op jit(solution)/shard_map/ppermute | solution.py:481
  43.5 2.9 %collective-permute-done.7.got3 = bf16[848,128]{1,0:T(8,128)(2,1)S(1)} collective-permute-done((bf16[848,128]{1,0:T(8,128)(2,1)S(1)}, bf16[848,128]{1,0:T(8,128)(2,1)S(1)}, u32[]{:S(2)}, u32[]{:S(2)}) %collective-permute-start.7) | collective-permute-done | bytes 217120 | tf_op jit(solution)/shard_map/ppermute | solution.py:481
  46.4 1.8 %collective-permute-done.8.got2 = bf16[848,128]{1,0:T(8,128)(2,1)S(1)} collective-permute-done((bf16[848,128]{1,0:T(8,128)(2,1)S(1)}, bf16[848,128]{1,0:T(8,128)(2,1)S(1)}, u32[]{:S(2)}, u32[]{:S(2)}) %collective-permute-start.8) | collective-permute-done | bytes 217120 | tf_op jit(solution)/shard_map/ppermute | solution.py:481
  48.2 0.7 %combine.1 = (f32[848,128]{1,0:T(8,128)S(1)}, bf16[528,128]{1,0:T(8,128)(2,1)S(1)}, bf16[272,128]{1,0:T(8,128)(2,1)S(1)}, bf16[528,128]{1,0:T(8,128)(2,1)S(1)}, bf16[272,128]{1,0:T(8,128)(2,1)S(1)}) custom-call(s32[128]{0:T(128)S(1)} %plan.1, f32[848,128]{1,0:T(8,128)S(1)} %get-tuple-element.17.keep, bf16[848,128]{1,0:T(8,128)(2,1)S(1)} %collective-permute-done.6.got1, ...), custom_call_target="tpu_custom_call" | custom-call | flops 1 | bytes 1 | tf_op jit(solution)/shard_map/combine/pallas_call | solution.py:418
  48.9 1.8 %collective-permute-start.9 = (bf16[528,128]{1,0:T(8,128)(2,1)S(1)}, bf16[528,128]{1,0:T(8,128)(2,1)S(1)}, u32[]{:S(2)}, u32[]{:S(2)}) collective-permute-start(bf16[528,128]{1,0:T(8,128)(2,1)S(1)} %get-tuple-element.22), channel_id=1, source_target_pairs={{0,64},{32,96},{64,0},{96,32},{1,65},{33,97},{65,1},{97,33},{2,66}... | collective-permute-start | bytes 405512 | tf_op jit(solution)/shard_map/ppermute | solution.py:481
  50.7 1.9 %collective-permute-start.10 = (bf16[528,128]{1,0:T(8,128)(2,1)S(1)}, bf16[528,128]{1,0:T(8,128)(2,1)S(1)}, u32[]{:S(2)}, u32[]{:S(2)}) collective-permute-start(bf16[528,128]{1,0:T(8,128)(2,1)S(1)} %get-tuple-element.23), channel_id=1, source_target_pairs={{0,1},{1,2},{2,3},{3,4},{4,5},{5,6},{6,7},{7,8},{8,9},{9,10},{10,1... | collective-permute-start | bytes 405512 | tf_op jit(solution)/shard_map/ppermute | solution.py:504
  52.6 1.1 %collective-permute-start.11 = (bf16[272,128]{1,0:T(8,128)(2,1)S(1)}, bf16[272,128]{1,0:T(8,128)(2,1)S(1)}, u32[]{:S(2)}, u32[]{:S(2)}) collective-permute-start(bf16[272,128]{1,0:T(8,128)(2,1)S(1)} %get-tuple-element.24), channel_id=1, source_target_pairs={{0,32},{32,0},{64,96},{96,64},{1,33},{33,1},{65,97},{97,65},{2,34}... | collective-permute-start | bytes 208904 | tf_op jit(solution)/shard_map/ppermute | solution.py:481
  53.7 4.5 %collective-permute-start.12 = (bf16[272,128]{1,0:T(8,128)(2,1)S(1)}, bf16[272,128]{1,0:T(8,128)(2,1)S(1)}, u32[]{:S(2)}, u32[]{:S(2)}) collective-permute-start(bf16[272,128]{1,0:T(8,128)(2,1)S(1)} %get-tuple-element.25), channel_id=1, source_target_pairs={{0,96},{32,64},{64,32},{96,0},{1,97},{33,65},{65,33},{97,1},{2,98}... | collective-permute-start | bytes 208904 | tf_op jit(solution)/shard_map/ppermute | solution.py:481
  58.2 0.0 collective-permute-done.11.got1
  58.2 2.6 %collective-permute-done.12.got3 = bf16[272,128]{1,0:T(8,128)(2,1)S(1)} collective-permute-done((bf16[272,128]{1,0:T(8,128)(2,1)S(1)}, bf16[272,128]{1,0:T(8,128)(2,1)S(1)}, u32[]{:S(2)}, u32[]{:S(2)}) %collective-permute-start.12) | collective-permute-done | bytes 69664 | tf_op jit(solution)/shard_map/ppermute | solution.py:481
  60.8 0.0 collective-permute-done.9.got2
  60.8 0.0 collective-permute-done.10.shifted
  60.8 1.9 %finish.1 = (f32[2,65,8,128]{3,2,1,0:T(8,128)}, f32[2,65,8,128]{3,2,1,0:T(8,128)}) custom-call(s32[128]{0:T(128)S(1)} %plan.1, f32[848,128]{1,0:T(8,128)S(1)} %get-tuple-element.21.full, bf16[528,128]{1,0:T(8,128)(2,1)S(1)} %collective-permute-done.9.got2, bf16[528,128]{1,0:T(8,128)(2,1)S(1)} %collective-permute-done.10.shifted, ...), custom_call_target="tpu_custom_call" | custom-call | flops 1 | bytes 1 | tf_op jit(solution)/shard_map/finish/pallas_call | solution.py:467
  (1 shorter events, 0.0 us)
Async XLA Ops:
  5.5 9.8 %copy-start.1 = (s32[2,8]{1,0:T(2,128)S(1)}, s32[2,8]{1,0:T(2,128)}, u32[]{:S(2)}) copy-start(s32[2,8]{1,0:T(2,128)} %param.4) | copy-start | bytes 196
  5.5 25.6 %copy-start = (bf16[512,256]{1,0:T(8,128)(2,1)S(1)}, bf16[512,256]{1,0:T(8,128)(2,1)}, u32[]{:S(2)}) copy-start(bf16[512,256]{1,0:T(8,128)(2,1)} %constant.2.clone.lag) | copy-start | bytes 786436
  5.6 25.6 %collective-permute-start.4 = (bf16[4,3,128,512]{3,2,1,0:T(8,128)(2,1)S(1)}, bf16[4,3,128,512]{3,2,1,0:T(8,128)(2,1)S(1)}, u32[]{:S(2)}, u32[]{:S(2)}) collective-permute-start(bf16[4,3,128,512]{3,2,1,0:T(8,128)(2,1)S(1)} %whiten.3.own_ext), channel_id=1, source_target_pairs={{1,2},{2,1},{3,4},{4,3},{5,6},{6,5},{7,8},{8,7},{9,10},{10,9},{11,... | collective-permute-start | bytes 4718600 | tf_op jit(solution)/shard_map/ppermute | solution.py:494
  15.2 15.9 %collective-permute-start.5 = (bf16[4,3,128,512]{3,2,1,0:T(8,128)(2,1)S(1)}, bf16[4,3,128,512]{3,2,1,0:T(8,128)(2,1)S(1)}, u32[]{:S(2)}, u32[]{:S(2)}) collective-permute-start(bf16[4,3,128,512]{3,2,1,0:T(8,128)(2,1)S(1)} %whiten.2.own_int), channel_id=1, source_target_pairs={{0,1},{1,0},{2,3},{3,2},{4,5},{5,4},{6,7},{7,6},{8,9},{9,8},{10,11... | collective-permute-start | bytes 4718600 | tf_op jit(solution)/shard_map/ppermute | solution.py:496
  15.3 5.5 %collective-permute-start.2 = (s32[2,8]{1,0:T(2,128)S(1)}, s32[2,8]{1,0:T(2,128)S(1)}, u32[]{:S(2)}, u32[]{:S(2)}) collective-permute-start(s32[2,8]{1,0:T(2,128)S(1)} %copy-done.1), channel_id=1, source_target_pairs={{0,64},{32,96},{64,0},{96,32},{1,65},{33,97},{65,1},{97,33},{2,66}... | collective-permute-start | bytes 200 | tf_op jit(solution)/shard_map/ppermute | solution.py:481
  19.3 4.8 %collective-permute-start.1 = (s32[2,8]{1,0:T(2,128)S(1)}, s32[2,8]{1,0:T(2,128)S(1)}, u32[]{:S(2)}, u32[]{:S(2)}) collective-permute-start(s32[2,8]{1,0:T(2,128)S(1)} %copy-done.1), channel_id=1, source_target_pairs={{0,96},{32,64},{64,32},{96,0},{1,97},{33,65},{65,33},{97,1},{2,98}... | collective-permute-start | bytes 200 | tf_op jit(solution)/shard_map/ppermute | solution.py:481
  20.0 4.1 %collective-permute-start = (s32[2,8]{1,0:T(2,128)S(1)}, s32[2,8]{1,0:T(2,128)S(1)}, u32[]{:S(2)}, u32[]{:S(2)}) collective-permute-start(s32[2,8]{1,0:T(2,128)S(1)} %copy-done.1), channel_id=1, source_target_pairs={{0,32},{32,0},{64,96},{96,64},{1,33},{33,1},{65,97},{97,65},{2,34}... | collective-permute-start | bytes 200 | tf_op jit(solution)/shard_map/ppermute | solution.py:481
  24.1 7.0 %collective-permute-start.3 = (s32[8,8]{1,0:T(8,128)S(1)}, s32[8,8]{1,0:T(8,128)S(1)}, u32[]{:S(2)}, u32[]{:S(2)}) collective-permute-start(s32[8,8]{1,0:T(8,128)S(1)} %pad_add_fusion.own), channel_id=1, source_target_pairs={{0,1},{1,2},{2,3},{3,4},{4,5},{5,6},{6,7},{7,8},{8,9},{9,10},{10,1... | collective-permute-start | bytes 776 | tf_op jit(solution)/shard_map/ppermute | solution.py:499
  35.8 7.7 %collective-permute-start.6 = (bf16[848,128]{1,0:T(8,128)(2,1)S(1)}, bf16[848,128]{1,0:T(8,128)(2,1)S(1)}, u32[]{:S(2)}, u32[]{:S(2)}) collective-permute-start(bf16[848,128]{1,0:T(8,128)(2,1)S(1)} %get-tuple-element.18), channel_id=1, source_target_pairs={{0,32},{32,0},{64,96},{96,64},{1,33},{33,1},{65,97},{97,65},{2,34}... | collective-permute-start | bytes 651272 | tf_op jit(solution)/shard_map/ppermute | solution.py:481
  36.2 10.2 %collective-permute-start.7 = (bf16[848,128]{1,0:T(8,128)(2,1)S(1)}, bf16[848,128]{1,0:T(8,128)(2,1)S(1)}, u32[]{:S(2)}, u32[]{:S(2)}) collective-permute-start(bf16[848,128]{1,0:T(8,128)(2,1)S(1)} %get-tuple-element.19), channel_id=1, source_target_pairs={{0,96},{32,64},{64,32},{96,0},{1,97},{33,65},{65,33},{97,1},{2,98}... | collective-permute-start | bytes 651272 | tf_op jit(solution)/shard_map/ppermute | solution.py:481
  38.7 9.4 %collective-permute-start.8 = (bf16[848,128]{1,0:T(8,128)(2,1)S(1)}, bf16[848,128]{1,0:T(8,128)(2,1)S(1)}, u32[]{:S(2)}, u32[]{:S(2)}) collective-permute-start(bf16[848,128]{1,0:T(8,128)(2,1)S(1)} %get-tuple-element.20), channel_id=1, source_target_pairs={{0,64},{32,96},{64,0},{96,32},{1,65},{33,97},{65,1},{97,33},{2,66}... | collective-permute-start | bytes 651272 | tf_op jit(solution)/shard_map/ppermute | solution.py:481
  48.9 11.9 %collective-permute-start.9 = (bf16[528,128]{1,0:T(8,128)(2,1)S(1)}, bf16[528,128]{1,0:T(8,128)(2,1)S(1)}, u32[]{:S(2)}, u32[]{:S(2)}) collective-permute-start(bf16[528,128]{1,0:T(8,128)(2,1)S(1)} %get-tuple-element.22), channel_id=1, source_target_pairs={{0,64},{32,96},{64,0},{96,32},{1,65},{33,97},{65,1},{97,33},{2,66}... | collective-permute-start | bytes 405512 | tf_op jit(solution)/shard_map/ppermute | solution.py:481
  50.7 10.1 %collective-permute-start.10 = (bf16[528,128]{1,0:T(8,128)(2,1)S(1)}, bf16[528,128]{1,0:T(8,128)(2,1)S(1)}, u32[]{:S(2)}, u32[]{:S(2)}) collective-permute-start(bf16[528,128]{1,0:T(8,128)(2,1)S(1)} %get-tuple-element.23), channel_id=1, source_target_pairs={{0,1},{1,2},{2,3},{3,4},{4,5},{5,6},{6,7},{7,8},{8,9},{9,10},{10,1... | collective-permute-start | bytes 405512 | tf_op jit(solution)/shard_map/ppermute | solution.py:504
  52.6 5.6 %collective-permute-start.11 = (bf16[272,128]{1,0:T(8,128)(2,1)S(1)}, bf16[272,128]{1,0:T(8,128)(2,1)S(1)}, u32[]{:S(2)}, u32[]{:S(2)}) collective-permute-start(bf16[272,128]{1,0:T(8,128)(2,1)S(1)} %get-tuple-element.24), channel_id=1, source_target_pairs={{0,32},{32,0},{64,96},{96,64},{1,33},{33,1},{65,97},{97,65},{2,34}... | collective-permute-start | bytes 208904 | tf_op jit(solution)/shard_map/ppermute | solution.py:481
  53.7 7.1 %collective-permute-start.12 = (bf16[272,128]{1,0:T(8,128)(2,1)S(1)}, bf16[272,128]{1,0:T(8,128)(2,1)S(1)}, u32[]{:S(2)}, u32[]{:S(2)}) collective-permute-start(bf16[272,128]{1,0:T(8,128)(2,1)S(1)} %get-tuple-element.25), channel_id=1, source_target_pairs={{0,96},{32,64},{64,32},{96,0},{1,97},{33,65},{65,33},{97,1},{2,98}... | collective-permute-start | bytes 208904 | tf_op jit(solution)/shard_map/ppermute | solution.py:481

commit v3 on v2

--- a/solution.py
+++ b/solution.py
@@ -108,12 +108,13 @@
     def load(k):
         return pltpu.make_async_copy(records.at[k, pl.ds(begin, ROWS)], buf.at[k], sems.at[k])
 
-    for k in range(segs):
-        load(k).start()
+    load(0).start()
     at = lax.broadcasted_iota(jnp.int32, (1, LENGTH), 1)
     count = jnp.minimum(at, SMOOTH) + jnp.minimum(LENGTH - 1 - at, SMOOTH) + 1
     share = 1.0 / count.astype(F32)
     make_tables(tab)
+    for k in range(1, segs):
+        load(k).start()
 
     def step(k, carry):
         load(k).wait()

time: 63 us -> 63.3 us (level)
  starting transfers between devices: 25.2 us -> 26.6 us
  waiting for transfers between devices: 18 us -> 17 us
    ppermute x9, starting transfers between devices: 16.6 us -> 18 us  [across(): return lax.ppermute(x, 'seg', [(z, z ^ r) for z in range(planes)])]
    ppermute x9, waiting for transfers between devices: 12.9 us -> 11.9 us  [across(): return lax.ppermute(x, 'seg', [(z, z ^ r) for z in range(planes)])]
where the time goes in v3:
time: 63.3 us; the launch traced here: 62.9 us
  starting transfers between devices  26.6 us (42%)
  Pallas kernels  18.5 us (29%)
  waiting for transfers between devices  17 us (27%)
  between operations  0.74 us (1%)
    ppermute x9, starting transfers between devices, across(): return lax.ppermute(x, 'seg', [(z, z ^ r) for z in range(planes)])  18 us
    ppermute x9, waiting for transfers between devices, across(): return lax.ppermute(x, 'seg', [(z, z ^ r) for z in range(planes)])  11.9 us
    pallas_call x2, Pallas kernels, whiten(): pl.pallas_call(functools.partial(whiten_body, outer), in_specs=[pl.BlockS...  9.78 us
    ppermute x1, waiting for transfers between devices, shards(): before = lax.ppermute(own, 'blk', upward)  5.11 us
    ppermute x1, starting transfers between devices, shards(): got_ext = lax.ppermute(own_ext, 'blk', outer)  4.76 us
    pallas_call x1, Pallas kernels, correlate(): pl.pallas_call(correlate_body, in_specs=[SMEM] * 2 + [VMEM] * 5, out_spec...  4.6 us
    ppermute x1, starting transfers between devices, shards(): before = lax.ppermute(own, 'blk', upward)  1.92 us
    ppermute x1, starting transfers between devices, shards(): shifted = lax.ppermute(send, ('seg', 'blk'), shift)  1.91 us
  transfers between devices with their start and end apart: 13, of which 7 were waited for; matrix products, arithmetic and copies ran while one was open for 0% of the time, Pallas kernels for 10%

profile of v3, /device:TPU:6, one launch (start us, length us, event | category | flops | bytes accessed | tf_op | source)
XLA Modules:
  0.0 62.9 jit_solution(8764934652692681850)
XLA Ops:
  0.6 4.9 %whiten.3.own_ext = bf16[4,3,128,512]{3,2,1,0:T(8,128)(2,1)S(1)} custom-call(f32[3,1024,512]{2,1,0:T(8,128)} %records.3), custom_call_target="tpu_custom_call" | custom-call | flops 1 | bytes 1 | tf_op jit(solution)/shard_map/whiten/pallas_call | solution.py:163
  5.5 0.0 copy-start.1
  5.5 0.0 copy-start
  5.6 4.8 %collective-permute-start.4 = (bf16[4,3,128,512]{3,2,1,0:T(8,128)(2,1)S(1)}, bf16[4,3,128,512]{3,2,1,0:T(8,128)(2,1)S(1)}, u32[]{:S(2)}, u32[]{:S(2)}) collective-permute-start(bf16[4,3,128,512]{3,2,1,0:T(8,128)(2,1)S(1)} %whiten.3.own_ext), channel_id=1, source_target_pairs={{1,2},{2,1},{3,4},{4,3},{5,6},{6,5},{7,8},{8,7},{9,10},{10,9},{11,... | collective-permute-start | bytes 4718600 | tf_op jit(solution)/shard_map/ppermute | solution.py:495
  10.3 4.9 %whiten.2.own_int = bf16[4,3,128,512]{3,2,1,0:T(8,128)(2,1)S(1)} custom-call(f32[3,1024,512]{2,1,0:T(8,128)} %records.3), custom_call_target="tpu_custom_call" | custom-call | flops 1 | bytes 1 | tf_op jit(solution)/shard_map/whiten/pallas_call | solution.py:163
  15.2 0.1 collective-permute-start.5
  15.3 0.0 copy-done.1
  15.3 4.0 %collective-permute-start.2 = (s32[2,8]{1,0:T(2,128)S(1)}, s32[2,8]{1,0:T(2,128)S(1)}, u32[]{:S(2)}, u32[]{:S(2)}) collective-permute-start(s32[2,8]{1,0:T(2,128)S(1)} %copy-done.1), channel_id=1, source_target_pairs={{0,64},{32,96},{64,0},{96,32},{1,65},{33,97},{65,1},{97,33},{2,66}... | collective-permute-start | bytes 200 | tf_op jit(solution)/shard_map/ppermute | solution.py:482
  19.3 0.7 %collective-permute-start.1 = (s32[2,8]{1,0:T(2,128)S(1)}, s32[2,8]{1,0:T(2,128)S(1)}, u32[]{:S(2)}, u32[]{:S(2)}) collective-permute-start(s32[2,8]{1,0:T(2,128)S(1)} %copy-done.1), channel_id=1, source_target_pairs={{0,96},{32,64},{64,32},{96,0},{1,97},{33,65},{65,33},{97,1},{2,98}... | collective-permute-start | bytes 200 | tf_op jit(solution)/shard_map/ppermute | solution.py:482
  20.0 0.3 collective-permute-start
  20.3 0.5 collective-permute-done.2
  20.8 3.2 %collective-permute-done.1 = s32[2,8]{1,0:T(2,128)S(1)} collective-permute-done((s32[2,8]{1,0:T(2,128)S(1)}, s32[2,8]{1,0:T(2,128)S(1)}, u32[]{:S(2)}, u32[]{:S(2)}) %collective-permute-start.1) | collective-permute-done | bytes 96 | tf_op jit(solution)/shard_map/ppermute | solution.py:482
  24.1 0.0 collective-permute-done
  24.1 1.9 %collective-permute-start.3 = (s32[8,8]{1,0:T(8,128)S(1)}, s32[8,8]{1,0:T(8,128)S(1)}, u32[]{:S(2)}, u32[]{:S(2)}) collective-permute-start(s32[8,8]{1,0:T(8,128)S(1)} %pad_add_fusion.own), channel_id=1, source_target_pairs={{0,1},{1,2},{2,3},{3,4},{4,5},{5,6},{6,7},{7,8},{8,9},{9,10},{10,1... | collective-permute-start | bytes 776 | tf_op jit(solution)/shard_map/ppermute | solution.py:500
  26.0 5.1 %collective-permute-done.3.before = s32[8,8]{1,0:T(8,128)S(1)} collective-permute-done((s32[8,8]{1,0:T(8,128)S(1)}, s32[8,8]{1,0:T(8,128)S(1)}, u32[]{:S(2)}, u32[]{:S(2)}) %collective-permute-start.3) | collective-permute-done | bytes 288 | tf_op jit(solution)/shard_map/ppermute | solution.py:500
  31.1 0.0 collective-permute-done.4.got_ext
  31.1 0.0 collective-permute-done.5.got_int
  31.1 0.0 copy-done
  31.1 4.6 %correlate.1 = (f32[848,128]{1,0:T(8,128)S(1)}, bf16[848,128]{1,0:T(8,128)(2,1)S(1)}, bf16[848,128]{1,0:T(8,128)(2,1)S(1)}, bf16[848,128]{1,0:T(8,128)(2,1)S(1)}, s32[128]{0:T(128)S(1)}) custom-call(s32[8,8]{1,0:T(8,128)S(1)} %pad_add_fusion.own, s32[8,8]{1,0:T(8,128)S(1)} %collective-permute-done.3.before, bf16[4,3,128,512]{3,2,1,0:T(8,128)(2,1)S(1)} %whiten.3.own_ext, ...), custom_call_target="tpu_custom_call" | custom-call | flops 1 | bytes 1 | tf_op jit(solution)/shard_map/correlate/pallas_call | solution.py:363
  35.7 0.5 collective-permute-start.6
  36.2 2.5 %collective-permute-start.7 = (bf16[848,128]{1,0:T(8,128)(2,1)S(1)}, bf16[848,128]{1,0:T(8,128)(2,1)S(1)}, u32[]{:S(2)}, u32[]{:S(2)}) collective-permute-start(bf16[848,128]{1,0:T(8,128)(2,1)S(1)} %get-tuple-element.19), channel_id=1, source_target_pairs={{0,96},{32,64},{64,32},{96,0},{1,97},{33,65},{65,33},{97,1},{2,98}... | collective-permute-start | bytes 651272 | tf_op jit(solution)/shard_map/ppermute | solution.py:482
  38.7 1.2 %collective-permute-start.8 = (bf16[848,128]{1,0:T(8,128)(2,1)S(1)}, bf16[848,128]{1,0:T(8,128)(2,1)S(1)}, u32[]{:S(2)}, u32[]{:S(2)}) collective-permute-start(bf16[848,128]{1,0:T(8,128)(2,1)S(1)} %get-tuple-element.20), channel_id=1, source_target_pairs={{0,64},{32,96},{64,0},{96,32},{1,65},{33,97},{65,1},{97,33},{2,66}... | collective-permute-start | bytes 651272 | tf_op jit(solution)/shard_map/ppermute | solution.py:482
  39.9 1.7 %plan.1 = s32[128]{0:T(128)S(1)} custom-call(s32[8,8]{1,0:T(8,128)S(1)} %pad_add_fusion.own, s32[8,8]{1,0:T(8,128)S(1)} %collective-permute-done.3.before, s32[128]{0:T(128)S(1)} %get-tuple-element.16.slots), custom_call_target="tpu_custom_call" | custom-call | flops 1 | bytes 1 | tf_op jit(solution)/shard_map/plan/pallas_call | solution.py:278
  41.6 0.6 collective-permute-done.6.got1
  42.2 2.9 %collective-permute-done.7.got3 = bf16[848,128]{1,0:T(8,128)(2,1)S(1)} collective-permute-done((bf16[848,128]{1,0:T(8,128)(2,1)S(1)}, bf16[848,128]{1,0:T(8,128)(2,1)S(1)}, u32[]{:S(2)}, u32[]{:S(2)}) %collective-permute-start.7) | collective-permute-done | bytes 217120 | tf_op jit(solution)/shard_map/ppermute | solution.py:482
  45.0 1.8 %collective-permute-done.8.got2 = bf16[848,128]{1,0:T(8,128)(2,1)S(1)} collective-permute-done((bf16[848,128]{1,0:T(8,128)(2,1)S(1)}, bf16[848,128]{1,0:T(8,128)(2,1)S(1)}, u32[]{:S(2)}, u32[]{:S(2)}) %collective-permute-start.8) | collective-permute-done | bytes 217120 | tf_op jit(solution)/shard_map/ppermute | solution.py:482
  46.8 0.7 %combine.1 = (f32[848,128]{1,0:T(8,128)S(1)}, bf16[528,128]{1,0:T(8,128)(2,1)S(1)}, bf16[272,128]{1,0:T(8,128)(2,1)S(1)}, bf16[528,128]{1,0:T(8,128)(2,1)S(1)}, bf16[272,128]{1,0:T(8,128)(2,1)S(1)}) custom-call(s32[128]{0:T(128)S(1)} %plan.1, f32[848,128]{1,0:T(8,128)S(1)} %get-tuple-element.17.keep, bf16[848,128]{1,0:T(8,128)(2,1)S(1)} %collective-permute-done.6.got1, ...), custom_call_target="tpu_custom_call" | custom-call | flops 1 | bytes 1 | tf_op jit(solution)/shard_map/combine/pallas_call | solution.py:419
  47.6 2.1 %collective-permute-start.9 = (bf16[528,128]{1,0:T(8,128)(2,1)S(1)}, bf16[528,128]{1,0:T(8,128)(2,1)S(1)}, u32[]{:S(2)}, u32[]{:S(2)}) collective-permute-start(bf16[528,128]{1,0:T(8,128)(2,1)S(1)} %get-tuple-element.22), channel_id=1, source_target_pairs={{0,64},{32,96},{64,0},{96,32},{1,65},{33,97},{65,1},{97,33},{2,66}... | collective-permute-start | bytes 405512 | tf_op jit(solution)/shard_map/ppermute | solution.py:482
  49.6 1.9 %collective-permute-start.10 = (bf16[528,128]{1,0:T(8,128)(2,1)S(1)}, bf16[528,128]{1,0:T(8,128)(2,1)S(1)}, u32[]{:S(2)}, u32[]{:S(2)}) collective-permute-start(bf16[528,128]{1,0:T(8,128)(2,1)S(1)} %get-tuple-element.23), channel_id=1, source_target_pairs={{0,1},{1,2},{2,3},{3,4},{4,5},{5,6},{6,7},{7,8},{8,9},{9,10},{10,1... | collective-permute-start | bytes 405512 | tf_op jit(solution)/shard_map/ppermute | solution.py:505
  51.5 0.8 %collective-permute-start.11 = (bf16[272,128]{1,0:T(8,128)(2,1)S(1)}, bf16[272,128]{1,0:T(8,128)(2,1)S(1)}, u32[]{:S(2)}, u32[]{:S(2)}) collective-permute-start(bf16[272,128]{1,0:T(8,128)(2,1)S(1)} %get-tuple-element.24), channel_id=1, source_target_pairs={{0,32},{32,0},{64,96},{96,64},{1,33},{33,1},{65,97},{97,65},{2,34}... | collective-permute-start | bytes 208904 | tf_op jit(solution)/shard_map/ppermute | solution.py:482
  52.4 5.9 %collective-permute-start.12 = (bf16[272,128]{1,0:T(8,128)(2,1)S(1)}, bf16[272,128]{1,0:T(8,128)(2,1)S(1)}, u32[]{:S(2)}, u32[]{:S(2)}) collective-permute-start(bf16[272,128]{1,0:T(8,128)(2,1)S(1)} %get-tuple-element.25), channel_id=1, source_target_pairs={{0,96},{32,64},{64,32},{96,0},{1,97},{33,65},{65,33},{97,1},{2,98}... | collective-permute-start | bytes 208904 | tf_op jit(solution)/shard_map/ppermute | solution.py:482
  58.3 0.0 collective-permute-done.11.got1
  58.3 2.9 %collective-permute-done.12.got3 = bf16[272,128]{1,0:T(8,128)(2,1)S(1)} collective-permute-done((bf16[272,128]{1,0:T(8,128)(2,1)S(1)}, bf16[272,128]{1,0:T(8,128)(2,1)S(1)}, u32[]{:S(2)}, u32[]{:S(2)}) %collective-permute-start.12) | collective-permute-done | bytes 69664 | tf_op jit(solution)/shard_map/ppermute | solution.py:482
  61.2 0.0 collective-permute-done.9.got2
  61.2 0.0 collective-permute-done.10.shifted
  61.2 1.8 %finish.1 = (f32[2,65,8,128]{3,2,1,0:T(8,128)}, f32[2,65,8,128]{3,2,1,0:T(8,128)}) custom-call(s32[128]{0:T(128)S(1)} %plan.1, f32[848,128]{1,0:T(8,128)S(1)} %get-tuple-element.21.full, bf16[528,128]{1,0:T(8,128)(2,1)S(1)} %collective-permute-done.9.got2, bf16[528,128]{1,0:T(8,128)(2,1)S(1)} %collective-permute-done.10.shifted, ...), custom_call_target="tpu_custom_call" | custom-call | flops 1 | bytes 1 | tf_op jit(solution)/shard_map/finish/pallas_call | solution.py:468
  (1 shorter events, 0.0 us)
Async XLA Ops:
  5.5 9.8 %copy-start.1 = (s32[2,8]{1,0:T(2,128)S(1)}, s32[2,8]{1,0:T(2,128)}, u32[]{:S(2)}) copy-start(s32[2,8]{1,0:T(2,128)} %param.4) | copy-start | bytes 196
  5.5 25.6 %copy-start = (bf16[512,256]{1,0:T(8,128)(2,1)S(1)}, bf16[512,256]{1,0:T(8,128)(2,1)}, u32[]{:S(2)}) copy-start(bf16[512,256]{1,0:T(8,128)(2,1)} %constant.2.clone.lag) | copy-start | bytes 786436
  5.6 25.6 %collective-permute-start.4 = (bf16[4,3,128,512]{3,2,1,0:T(8,128)(2,1)S(1)}, bf16[4,3,128,512]{3,2,1,0:T(8,128)(2,1)S(1)}, u32[]{:S(2)}, u32[]{:S(2)}) collective-permute-start(bf16[4,3,128,512]{3,2,1,0:T(8,128)(2,1)S(1)} %whiten.3.own_ext), channel_id=1, source_target_pairs={{1,2},{2,1},{3,4},{4,3},{5,6},{6,5},{7,8},{8,7},{9,10},{10,9},{11,... | collective-permute-start | bytes 4718600 | tf_op jit(solution)/shard_map/ppermute | solution.py:495
  15.2 15.9 %collective-permute-start.5 = (bf16[4,3,128,512]{3,2,1,0:T(8,128)(2,1)S(1)}, bf16[4,3,128,512]{3,2,1,0:T(8,128)(2,1)S(1)}, u32[]{:S(2)}, u32[]{:S(2)}) collective-permute-start(bf16[4,3,128,512]{3,2,1,0:T(8,128)(2,1)S(1)} %whiten.2.own_int), channel_id=1, source_target_pairs={{0,1},{1,0},{2,3},{3,2},{4,5},{5,4},{6,7},{7,6},{8,9},{9,8},{10,11... | collective-permute-start | bytes 4718600 | tf_op jit(solution)/shard_map/ppermute | solution.py:497
  15.3 5.5 %collective-permute-start.2 = (s32[2,8]{1,0:T(2,128)S(1)}, s32[2,8]{1,0:T(2,128)S(1)}, u32[]{:S(2)}, u32[]{:S(2)}) collective-permute-start(s32[2,8]{1,0:T(2,128)S(1)} %copy-done.1), channel_id=1, source_target_pairs={{0,64},{32,96},{64,0},{96,32},{1,65},{33,97},{65,1},{97,33},{2,66}... | collective-permute-start | bytes 200 | tf_op jit(solution)/shard_map/ppermute | solution.py:482
  19.3 4.8 %collective-permute-start.1 = (s32[2,8]{1,0:T(2,128)S(1)}, s32[2,8]{1,0:T(2,128)S(1)}, u32[]{:S(2)}, u32[]{:S(2)}) collective-permute-start(s32[2,8]{1,0:T(2,128)S(1)} %copy-done.1), channel_id=1, source_target_pairs={{0,96},{32,64},{64,32},{96,0},{1,97},{33,65},{65,33},{97,1},{2,98}... | collective-permute-start | bytes 200 | tf_op jit(solution)/shard_map/ppermute | solution.py:482
  20.0 4.1 %collective-permute-start = (s32[2,8]{1,0:T(2,128)S(1)}, s32[2,8]{1,0:T(2,128)S(1)}, u32[]{:S(2)}, u32[]{:S(2)}) collective-permute-start(s32[2,8]{1,0:T(2,128)S(1)} %copy-done.1), channel_id=1, source_target_pairs={{0,32},{32,0},{64,96},{96,64},{1,33},{33,1},{65,97},{97,65},{2,34}... | collective-permute-start | bytes 200 | tf_op jit(solution)/shard_map/ppermute | solution.py:482
  24.1 7.0 %collective-permute-start.3 = (s32[8,8]{1,0:T(8,128)S(1)}, s32[8,8]{1,0:T(8,128)S(1)}, u32[]{:S(2)}, u32[]{:S(2)}) collective-permute-start(s32[8,8]{1,0:T(8,128)S(1)} %pad_add_fusion.own), channel_id=1, source_target_pairs={{0,1},{1,2},{2,3},{3,4},{4,5},{5,6},{6,7},{7,8},{8,9},{9,10},{10,1... | collective-permute-start | bytes 776 | tf_op jit(solution)/shard_map/ppermute | solution.py:500
  35.7 6.4 %collective-permute-start.6 = (bf16[848,128]{1,0:T(8,128)(2,1)S(1)}, bf16[848,128]{1,0:T(8,128)(2,1)S(1)}, u32[]{:S(2)}, u32[]{:S(2)}) collective-permute-start(bf16[848,128]{1,0:T(8,128)(2,1)S(1)} %get-tuple-element.18), channel_id=1, source_target_pairs={{0,32},{32,0},{64,96},{96,64},{1,33},{33,1},{65,97},{97,65},{2,34}... | collective-permute-start | bytes 651272 | tf_op jit(solution)/shard_map/ppermute | solution.py:482
  36.2 8.9 %collective-permute-start.7 = (bf16[848,128]{1,0:T(8,128)(2,1)S(1)}, bf16[848,128]{1,0:T(8,128)(2,1)S(1)}, u32[]{:S(2)}, u32[]{:S(2)}) collective-permute-start(bf16[848,128]{1,0:T(8,128)(2,1)S(1)} %get-tuple-element.19), channel_id=1, source_target_pairs={{0,96},{32,64},{64,32},{96,0},{1,97},{33,65},{65,33},{97,1},{2,98}... | collective-permute-start | bytes 651272 | tf_op jit(solution)/shard_map/ppermute | solution.py:482
  38.7 8.1 %collective-permute-start.8 = (bf16[848,128]{1,0:T(8,128)(2,1)S(1)}, bf16[848,128]{1,0:T(8,128)(2,1)S(1)}, u32[]{:S(2)}, u32[]{:S(2)}) collective-permute-start(bf16[848,128]{1,0:T(8,128)(2,1)S(1)} %get-tuple-element.20), channel_id=1, source_target_pairs={{0,64},{32,96},{64,0},{96,32},{1,65},{33,97},{65,1},{97,33},{2,66}... | collective-permute-start | bytes 651272 | tf_op jit(solution)/shard_map/ppermute | solution.py:482
  47.6 13.6 %collective-permute-start.9 = (bf16[528,128]{1,0:T(8,128)(2,1)S(1)}, bf16[528,128]{1,0:T(8,128)(2,1)S(1)}, u32[]{:S(2)}, u32[]{:S(2)}) collective-permute-start(bf16[528,128]{1,0:T(8,128)(2,1)S(1)} %get-tuple-element.22), channel_id=1, source_target_pairs={{0,64},{32,96},{64,0},{96,32},{1,65},{33,97},{65,1},{97,33},{2,66}... | collective-permute-start | bytes 405512 | tf_op jit(solution)/shard_map/ppermute | solution.py:482
  49.6 11.5 %collective-permute-start.10 = (bf16[528,128]{1,0:T(8,128)(2,1)S(1)}, bf16[528,128]{1,0:T(8,128)(2,1)S(1)}, u32[]{:S(2)}, u32[]{:S(2)}) collective-permute-start(bf16[528,128]{1,0:T(8,128)(2,1)S(1)} %get-tuple-element.23), channel_id=1, source_target_pairs={{0,1},{1,2},{2,3},{3,4},{4,5},{5,6},{6,7},{7,8},{8,9},{9,10},{10,1... | collective-permute-start | bytes 405512 | tf_op jit(solution)/shard_map/ppermute | solution.py:505
  51.5 6.8 %collective-permute-start.11 = (bf16[272,128]{1,0:T(8,128)(2,1)S(1)}, bf16[272,128]{1,0:T(8,128)(2,1)S(1)}, u32[]{:S(2)}, u32[]{:S(2)}) collective-permute-start(bf16[272,128]{1,0:T(8,128)(2,1)S(1)} %get-tuple-element.24), channel_id=1, source_target_pairs={{0,32},{32,0},{64,96},{96,64},{1,33},{33,1},{65,97},{97,65},{2,34}... | collective-permute-start | bytes 208904 | tf_op jit(solution)/shard_map/ppermute | solution.py:482
  52.4 8.8 %collective-permute-start.12 = (bf16[272,128]{1,0:T(8,128)(2,1)S(1)}, bf16[272,128]{1,0:T(8,128)(2,1)S(1)}, u32[]{:S(2)}, u32[]{:S(2)}) collective-permute-start(bf16[272,128]{1,0:T(8,128)(2,1)S(1)} %get-tuple-element.25), channel_id=1, source_target_pairs={{0,96},{32,64},{64,32},{96,0},{1,97},{33,65},{65,33},{97,1},{2,98}... | collective-permute-start | bytes 208904 | tf_op jit(solution)/shard_map/ppermute | solution.py:482
